TPU v7x, 128 devices: a whole 4x4x4 slice. The times are simulated.
128 devices in a mesh: seq: 64 (over y, z_hi, x, core), shard: 2 (over z_lo).
Axes of the slice: x: 4, y: 4, z: 4 (z_hi: 2, z_lo: 2; z = z_hi * 2 + z_lo), core: 2. Of those that a mesh axis runs over, the one named last changes fastest.
Arguments:
- tokens: bfloat16 [32768, 1024], P('seq', 'shard'), may hold values from -16 to 16
- norm_gain: bfloat16 [1024], replicated, may hold values from 0.099609375 to 1.8984375
- in_weight: bfloat16 [1024, 3, 1024], P(None, None, 'shard'), may hold values from -0.1875 to 0.1875
- conv_weight: bfloat16 [3, 1024], P(None, 'shard'), may hold values from -3 to 3
- out_weight: bfloat16 [1024, 1024], P('shard'), may hold values from -0.1875 to 0.1875
- ffn_gain: bfloat16 [1024], replicated, may hold values from 0.099609375 to 1.8984375
- gate_weight: bfloat16 [1024, 4608], P(None, 'shard'), may hold values from -0.1875 to 0.1875
- up_weight: bfloat16 [1024, 4608], P(None, 'shard'), may hold values from -0.1875 to 0.1875
- down_weight: bfloat16 [4608, 1024], P('shard'), may hold values from -0.1875 to 0.1875
- cotangent: bfloat16 [32768, 1024], P('seq', 'shard'), may hold values from -16 to 16
Outputs:
- block_out: bfloat16 [32768, 1024], P('seq', 'shard')
- token_grad: float32 [32768, 1024], P('seq', 'shard')
- norm_gain_grad: float32 [1024], replicated
- in_weight_grad: float32 [1024, 3, 1024], P('seq', None, 'shard')
- conv_weight_grad: float32 [3, 1024], P(None, 'shard')
- out_weight_grad: float32 [1024, 1024], P('shard', 'seq')
- ffn_gain_grad: float32 [1024], replicated
- gate_weight_grad: float32 [1024, 4608], P('seq', 'shard')
- up_weight_grad: float32 [1024, 4608], P('seq', 'shard')
- down_weight_grad: float32 [4608, 1024], P('shard', 'seq')
All inputs are finite; a program needn't handle non-finite values.
Results may differ from a plain program's by a relative error of at most 0.018.
Values may be sent and summed in bfloat16 or wider, within the bound.
A program may use at most 192 MiB of HBM per device.

v0:
```python
import math

import jax
import jax.numpy as jnp
from jax import lax
from jax.sharding import PartitionSpec as P

SEQS = 2


NORM_EPS = 1e-05


def sent_to_all(array, axis):
    length = lax.axis_size(axis)
    return lax.all_to_all(
        jnp.broadcast_to(array[None], (length, *array.shape)), axis, 0, 0, tiled=True
    )


def laid_out(blocks, dim):
    shape = list(blocks.shape[1:])
    shape[dim] *= blocks.shape[0]
    return jnp.moveaxis(blocks, 0, dim).reshape(shape)


def gather_directly(array, axis, dim):
    blocks = sent_to_all(array, axis)
    return laid_out(blocks, dim)


def shifted(block, axis, distance):
    devices = range(lax.axis_size(axis))
    route = [(i - distance, i) for i in devices if i - distance in devices]
    return lax.ppermute(block, axis, route)


def of_everyone(array, axis):
    everything = sent_to_all(array, axis)
    return jnp.sum(everything.astype(jnp.float32), axis=0)


def split_up(array, dim, length):
    before, after = (array.shape[:dim], array.shape[dim + 1 :])
    return jnp.moveaxis(array.reshape(*before, length, -1, *after), dim, 0)


def sent_and_summed(array, axis, dim):
    blocks = split_up(array, dim, lax.axis_size(axis))
    arrived = lax.all_to_all(blocks, axis, split_axis=0, concat_axis=0, tiled=True)
    return arrived.astype(jnp.float32).sum(axis=0)


def over_copies(array, axis):
    everything = sent_to_all(array, axis)
    return jnp.sum(everything, axis=0)


def packed_total(arrays, axis):
    ends = [0]
    for a in arrays:
        ends.append(ends[-1] + a.size)
    so_far = over_copies(jnp.concatenate([a.ravel() for a in arrays]), axis)
    return tuple((so_far[b:e].reshape(a.shape) for a, b, e in zip(arrays, ends, ends[1:])))


def side_by_side(arrays, axis, dim, along):
    widths = [math.prod(a.shape[along:]) for a in arrays]
    both = jnp.concatenate(
        [a.reshape(*a.shape[:along], w) for a, w in zip(arrays, widths)], axis=along
    )
    whole = lax.psum_scatter(both, axis, scatter_dimension=dim, tiled=True)
    blocks = jnp.split(whole, [sum(widths[:k]) for k in range(1, len(widths))], axis=along)
    return tuple(
        (b.reshape(*whole.shape[:along], *a.shape[along:]) for a, b in zip(arrays, blocks))
    )


def body(
    tokens,
    norm_gain,
    in_weight,
    conv_weight,
    out_weight,
    ffn_gain,
    gate_weight,
    up_weight,
    down_weight,
    cotangent,
):
    f32 = jnp.float32
    bf16 = jnp.bfloat16
    row_count = tokens.shape[0]
    half_cols = tokens.shape[1]
    shard_start = lax.axis_index("shard") * half_cols
    whole_in = gather_directly(tokens, "shard", 1)
    x_full = whole_in.astype(f32)
    gain_one = norm_gain.astype(f32)
    gain_two = ffn_gain.astype(f32)
    inv_one = lax.rsqrt(jnp.mean(x_full * x_full, axis=-1, keepdims=True) + NORM_EPS)
    normed_in = (x_full * inv_one * gain_one).astype(bf16)
    w_in_flat = in_weight.reshape(in_weight.shape[0], -1)
    projected = jnp.dot(normed_in, w_in_flat, preferred_element_type=f32).reshape(
        row_count, 3, half_cols
    )
    b_gate = projected[:, 0]
    c_gate = projected[:, 1]
    x_gate = projected[:, 2]
    gated = b_gate * x_gate
    per_seq = lax.axis_size("seq") // SEQS
    seq_start = lax.axis_index("seq") % per_seq == 0
    carry_mask = jnp.where(seq_start, 0.0, 1.0).astype(f32)
    before = shifted(gated[-2:], "seq", 1) * carry_mask
    extended = jnp.concatenate([before, gated], axis=0)
    kernel = conv_weight.astype(f32)
    conv_out = kernel[0] * extended[:-2] + kernel[1] * extended[1:-1] + kernel[2] * extended[2:]
    mixed_in = (c_gate * conv_out).astype(bf16)
    mixer_terms = jnp.dot(mixed_in, out_weight, preferred_element_type=f32)
    stream_full = x_full + of_everyone(mixer_terms.astype(jnp.bfloat16), "shard").astype(
        jnp.float32
    )
    stream_own = lax.dynamic_slice_in_dim(stream_full, shard_start, half_cols, 1)
    inv_two = lax.rsqrt(jnp.mean(stream_full * stream_full, axis=-1, keepdims=True) + NORM_EPS)
    normed_mid = (stream_full * inv_two * gain_two).astype(bf16)
    gate_pre = jnp.dot(normed_mid, gate_weight, preferred_element_type=f32)
    up_pre = jnp.dot(normed_mid, up_weight, preferred_element_type=f32)
    sigmoid_gate = jax.nn.sigmoid(gate_pre)
    silu_gate = gate_pre * sigmoid_gate
    hidden = (silu_gate * up_pre).astype(bf16)
    ffn_terms = jnp.dot(hidden, down_weight, preferred_element_type=f32)
    block_out = (stream_own + sent_and_summed(ffn_terms.astype(jnp.bfloat16), "shard", 1)).astype(
        bf16
    )
    cot_full = gather_directly(cotangent, "shard", 1)
    down_local = jnp.einsum("tf,td->fd", hidden, cot_full, preferred_element_type=f32)
    d_hidden = jnp.einsum("td,fd->tf", cot_full, down_weight, preferred_element_type=f32)
    d_gate = (d_hidden * up_pre * sigmoid_gate * (1.0 + gate_pre * (1.0 - sigmoid_gate))).astype(
        bf16
    )
    d_up = (d_hidden * silu_gate).astype(bf16)
    gate_local = jnp.einsum("tk,tf->kf", normed_mid, d_gate, preferred_element_type=f32)
    up_local = jnp.einsum("tk,tf->kf", normed_mid, d_up, preferred_element_type=f32)
    d_mid_terms = jnp.einsum("tf,kf->tk", d_gate, gate_weight, preferred_element_type=f32)
    d_mid_terms = d_mid_terms + jnp.einsum("tf,kf->tk", d_up, up_weight, preferred_element_type=f32)
    d_normed_mid = of_everyone(d_mid_terms.astype(jnp.bfloat16), "shard").astype(jnp.float32)
    ffn_gain_local = jnp.sum(d_normed_mid * stream_full * inv_two, axis=0)
    scaled_mid = d_normed_mid * gain_two
    d_stream = (
        cot_full.astype(f32)
        + inv_two * scaled_mid
        - stream_full * inv_two**3 * jnp.mean(scaled_mid * stream_full, axis=-1, keepdims=True)
    )
    d_stream_low = d_stream.astype(bf16)
    out_local = jnp.einsum("tc,td->cd", mixed_in, d_stream_low, preferred_element_type=f32)
    d_mixed_in = jnp.einsum("td,cd->tc", d_stream_low, out_weight, preferred_element_type=f32)
    d_c_gate = d_mixed_in * conv_out
    d_conv = d_mixed_in * c_gate
    conv_local = jnp.stack(
        [
            jnp.sum(d_conv * extended[:-2], axis=0),
            jnp.sum(d_conv * extended[1:-1], axis=0),
            jnp.sum(d_conv * extended[2:], axis=0),
        ],
        axis=0,
    )
    d_extended = (
        jnp.pad(kernel[0] * d_conv, ((0, 2), (0, 0)))
        + jnp.pad(kernel[1] * d_conv, ((1, 1), (0, 0)))
        + jnp.pad(kernel[2] * d_conv, ((2, 0), (0, 0)))
    )
    sent_back = d_extended[:2] * carry_mask
    from_next = shifted(sent_back, "seq", -1)
    d_gated = d_extended[2:] + jnp.concatenate(
        [jnp.zeros((row_count - 2, half_cols), f32), from_next], axis=0
    )
    d_projected = jnp.stack([d_gated * x_gate, d_c_gate, d_gated * b_gate], axis=1).astype(bf16)
    flat_dproj = d_projected.reshape(row_count, -1)
    in_local = jnp.einsum("tk,tj->kj", normed_in, flat_dproj, preferred_element_type=f32).reshape(
        in_weight.shape
    )
    d_in_terms = jnp.einsum("tj,kj->tk", flat_dproj, w_in_flat, preferred_element_type=f32)
    d_normed_in = of_everyone(d_in_terms.astype(jnp.bfloat16), "shard").astype(jnp.float32)
    norm_gain_local = jnp.sum(d_normed_in * x_full * inv_one, axis=0)
    scaled_in = d_normed_in * gain_one
    d_input_full = (
        d_stream
        + inv_one * scaled_in
        - x_full * inv_one**3 * jnp.mean(scaled_in * x_full, axis=-1, keepdims=True)
    )
    token_grad = lax.dynamic_slice_in_dim(d_input_full, shard_start, half_cols, 1)
    conv_grad, norm_gain_grad, ffn_gain_grad = packed_total(
        (conv_local, norm_gain_local, ffn_gain_local), "seq"
    )
    in_grad, gate_grad, up_grad, out_turned, down_turned = side_by_side(
        (in_local, gate_local, up_local, out_local.T, down_local.T), "seq", 0, 1
    )
    out_grad = out_turned.T
    down_grad = down_turned.T
    return (
        block_out,
        token_grad,
        norm_gain_grad,
        in_grad,
        conv_grad,
        out_grad,
        ffn_gain_grad,
        gate_grad,
        up_grad,
        down_grad,
    )


def solution(mesh):
    return jax.shard_map(
        body,
        mesh=mesh,
        in_specs=(
            P("seq", "shard"),
            P(),
            P(None, None, "shard"),
            P(None, "shard"),
            P("shard", None),
            P(),
            P(None, "shard"),
            P(None, "shard"),
            P("shard", None),
            P("seq", "shard"),
        ),
        out_specs=(
            P("seq", "shard"),
            P("seq", "shard"),
            P(),
            P("seq", None, "shard"),
            P(None, "shard"),
            P("shard", "seq"),
            P(),
            P("seq", "shard"),
            P("seq", "shard"),
            P("shard", "seq"),
        ),
        check_vma=False,
    )
```

profile of v0, /device:TPU:0, one launch (start us, length us, event | category | flops | bytes accessed | tf_op | source)
XLA Modules:
  0.0 617.1 jit_solution(14835222997066530516)
XLA Ops:
  9.4 3.6 all-to-all-start
  13.0 4.7 copy.76
  17.7 9.4 %all-to-all-done = bf16[2,512,512]{2,1,0:T(8,128)(2,1)S(1)} async-done(((bf16[2,512,512]{2,1,0:T(8,128)(2,1)}), bf16[2,512,512]{2,1,0:T(8,128)(2,1)S(1)}, u32[]{:S(2)}, u32[]{:S(2)}) %all-to-all-start) | async-done | bytes 1048608 | tf_op jit(solution)/shard_map/all_to_all | solution.py:16
  28.2 4.4 all-to-all-start.3
  49.3 5.2 all-to-all-start.1
  61.3 17.8 %all-to-all-done.1 = bf16[2,512,1024]{2,1,0:T(8,128)(2,1)} async-done(((bf16[2,512,1024]{2,1,0:T(8,128)(2,1)}), bf16[2,512,1024]{2,1,0:T(8,128)(2,1)}, u32[]{:S(2)}, u32[]{:S(2)}) %all-to-all-start.1) | async-done | bytes 2097184 | tf_op jit(solution)/shard_map/all_to_all | solution.py:16
  79.2 3.6 convert_reduce_fusion.2
  82.8 2.9 copy.79
  87.9 3.5 multiply_convert_fusion.3
  91.4 7.1 %fusion.25 = f32[512,2304]{1,0:T(8,128)} fusion(bf16[512,1024]{1,0:T(8,128)(2,1)S(1)} %get-tuple-element.87, bf16[1024,2304]{1,0:T(8,128)(2,1)} %param.17), kind=kOutput, calls=%fused_computation.89 | convolution fusion | flops 2415919104 | bytes 10485760 | tf_op jit(solution)/shard_map/dot_general | solution.py:126
  98.5 4.3 fusion.24
  102.8 9.9 %multiply_convert_fusion = (bf16[512,2304]{1,0:T(8,128)(2,1)S(1)}, bf16[512,2304]{1,0:T(8,128)(2,1)}, bf16[512,2304]{1,0:T(8,128)(2,1)}) fusion(f32[512,2304]{1,0:T(8,128)} %fusion.24, f32[512,2304]{1,0:T(8,128)} %fusion.25, bf16[512,1024]{0,1:T(8,128)(2,1)S(1)} %bitcast.136, bf16[2304,1024]{1,0:T(8,128)(2,1)} %param.18), kind=kOutput, calls=%fused_computation.4 | convolution fusion | flops 2433613824 | bytes 22282240 | tf_op jit(solution)/shard_map/td,fd->tf/dot_general | solution.py:136
  112.7 5.1 fusion.26
  122.1 4.8 all-to-all-start.4
  129.5 23.5 %all-to-all-done.4 = bf16[2,512,1024]{2,1,0:T(8,128)(2,1)} async-done(((bf16[2,512,1024]{2,1,0:T(8,128)(2,1)}), bf16[2,512,1024]{2,1,0:T(8,128)(2,1)}, u32[]{:S(2)}, u32[]{:S(2)}) %all-to-all-start.4) | async-done | bytes 2097184 | tf_op jit(solution)/shard_map/all_to_all | solution.py:16
  153.0 3.6 convert_reduce_fusion.1
  156.6 2.9 copy.83
  175.2 6.1 convolution_dynamic-update-slice_fusion.2
  181.3 5.1 convolution_dynamic-update-slice_fusion.1
  186.4 5.1 convolution_dynamic-update-slice_fusion
  194.2 5.2 bitcast_dynamic-update-slice_fusion
  200.4 3.7 bitcast_convert_fusion
  205.7 4.8 all-to-all-start.5
  210.6 5.7 convolution_convert_fusion
  217.3 45.4 %all-to-all-done.5 = bf16[2,512,1024]{2,1,0:T(8,128)(2,1)} async-done(((bf16[2,512,1024]{2,1,0:T(8,128)(2,1)}), bf16[2,512,1024]{2,1,0:T(8,128)(2,1)}, u32[]{:S(2)}, u32[]{:S(2)}) %all-to-all-start.5) | async-done | bytes 2097184 | tf_op jit(solution)/shard_map/all_to_all | solution.py:16
  262.7 3.9 all-to-all-start.2
  266.6 3.6 convert_reduce_fusion
  273.0 4.6 fusion.4
  277.7 19.6 %all-to-all-done.2 = bf16[2,512,512]{2,1,0:T(8,128)(2,1)S(1)} async-done(((bf16[2,512,512]{2,1,0:T(8,128)(2,1)}), bf16[2,512,512]{2,1,0:T(8,128)(2,1)S(1)}, u32[]{:S(2)}, u32[]{:S(2)}) %all-to-all-start.2) | async-done | bytes 1048608 | tf_op jit(solution)/shard_map/all_to_all | solution.py:50
  298.7 18.6 %all-to-all-start.6 = ((f32[64,1,3584]{2,1,0:T(1,128)}), f32[64,1,3584]{2,1,0:T(1,128)}, u32[]{:S(2)}, u32[]{:S(2)}) async-start(f32[64,1,3584]{2,1,0:T(1,128)} %broadcast_in_dim.17), calls=%async_computation.6 | async-start | bytes 1835008 | tf_op jit(solution)/shard_map/all_to_all | solution.py:16
  322.4 17.6 %all-to-all-done.6 = f32[64,1,3584]{2,1,0:T(1,128)} async-done(((f32[64,1,3584]{2,1,0:T(1,128)}), f32[64,1,3584]{2,1,0:T(1,128)}, u32[]{:S(2)}, u32[]{:S(2)}) %all-to-all-start.6) | async-done | bytes 917536 | tf_op jit(solution)/shard_map/all_to_all | solution.py:16
  343.0 262.5 %reduce-scatter.2.cloned.1.call-done = f32[16,8960]{1,0:T(8,128)} async-done(((f32[1024,8960]{1,0:T(8,128)}), f32[16,8960]{1,0:T(8,128)}) %reduce-scatter.2.cloned.1.call-update) | async-done | bytes 573456 | tf_op jit(solution)/shard_map/reduce_scatter | solution.py:72
  (142 shorter events, 74.7 us)
Async XLA Ops:
  7.2 37.5 %copy-start = (bf16[512,1024]{1,0:T(8,128)(2,1)S(1)}, bf16[512,1024]{1,0:T(8,128)(2,1)}, u32[]{:S(2)}) copy-start(bf16[512,1024]{1,0:T(8,128)(2,1)} %param.14) | copy-start | bytes 3145732
  7.2 5.8 copy-start.28
  9.4 17.7 %all-to-all-start = ((bf16[2,512,512]{2,1,0:T(8,128)(2,1)}), bf16[2,512,512]{2,1,0:T(8,128)(2,1)S(1)}, u32[]{:S(2)}, u32[]{:S(2)}) async-start(bf16[2,512,512]{2,1,0:T(8,128)(2,1)} %broadcast_in_dim.12), calls=%async_computation | async-start | bytes 2097152 | tf_op jit(solution)/shard_map/all_to_all | solution.py:16
  13.0 14.1 %copy-start.25 = (bf16[512,512]{1,0:T(8,128)(2,1)S(1)}, bf16[512,512]{1,0:T(8,128)(2,1)}, u32[]{:S(2)}) copy-start(bf16[512,512]{1,0:T(8,128)(2,1)} %param.19) | copy-start | bytes 1572868
  28.2 18.2 %all-to-all-start.3 = ((bf16[2,512,512]{2,1,0:T(8,128)(2,1)}), bf16[2,512,512]{2,1,0:T(8,128)(2,1)}, u32[]{:S(2)}, u32[]{:S(2)}) async-start(bf16[2,512,512]{2,1,0:T(8,128)(2,1)} %broadcast_in_dim.14), calls=%async_computation.3 | async-start | bytes 2097152 | tf_op jit(solution)/shard_map/all_to_all | solution.py:16
  33.8 3.5 copy-start.21
  39.2 2.1 collective-permute-start
  49.3 5.2 copy-start.27
  49.3 29.9 %all-to-all-start.1 = ((bf16[2,512,1024]{2,1,0:T(8,128)(2,1)}), bf16[2,512,1024]{2,1,0:T(8,128)(2,1)}, u32[]{:S(2)}, u32[]{:S(2)}) async-start(bf16[2,512,1024]{2,1,0:T(8,128)(2,1)} %broadcast_in_dim.13), calls=%async_computation.1 | async-start | bytes 4194304 | tf_op jit(solution)/shard_map/all_to_all | solution.py:16
  87.9 10.6 %slice-start = ((s8[4718592]{0:T(1024)(128)(4,1)}), s8[4194304]{0:T(1024)(128)(4,1)S(1)}, s32[]{:S(2)}) async-start(s8[4718592]{0:T(1024)(128)(4,1)} %bitcast.157), calls=%async_computation.9 | async-start | bytes 8388608
  91.4 7.1 %copy-start.23 = (bf16[512,1024]{1,0:T(8,128)(2,1)}, bf16[512,1024]{1,0:T(8,128)(2,1)S(1)}, u32[]{:S(2)}) copy-start(bf16[512,1024]{1,0:T(8,128)(2,1)S(1)} %get-tuple-element.87) | copy-start | bytes 3145732
  91.4 7.1 %slice-start.1 = ((s8[4718592]{0:T(1024)(128)(4,1)}), s8[524288]{0:T(1024)(128)(4,1)S(1)}, s32[]{:S(2)}) async-start(s8[4718592]{0:T(1024)(128)(4,1)} %bitcast.157), calls=%async_computation.10 | async-start | bytes 1048576
  98.5 4.3 copy-start.13
  98.5 19.4 %slice-start.2 = ((s8[4718592]{0:T(1024)(128)(4,1)}), s8[4194304]{0:T(1024)(128)(4,1)S(1)}, s32[]{:S(2)}) async-start(s8[4718592]{0:T(1024)(128)(4,1)} %bitcast.159), calls=%async_computation.11 | async-start | bytes 8388608
  102.8 15.1 %slice-start.3 = ((s8[4718592]{0:T(1024)(128)(4,1)}), s8[524288]{0:T(1024)(128)(4,1)S(1)}, s32[]{:S(2)}) async-start(s8[4718592]{0:T(1024)(128)(4,1)} %bitcast.159), calls=%async_computation.12 | async-start | bytes 1048576
  112.7 5.1 copy-start.29
  122.1 30.9 %all-to-all-start.4 = ((bf16[2,512,1024]{2,1,0:T(8,128)(2,1)}), bf16[2,512,1024]{2,1,0:T(8,128)(2,1)}, u32[]{:S(2)}, u32[]{:S(2)}) async-start(bf16[2,512,1024]{2,1,0:T(8,128)(2,1)} %broadcast_in_dim.15), calls=%async_computation.4 | async-start | bytes 4194304 | tf_op jit(solution)/shard_map/all_to_all | solution.py:16
  126.9 478.6 %reduce-scatter.2.cloned.1.call-start = ((), (), s32[]{:S(2)}) async-start(), calls=%async_computation.8 | async-start | bytes 37273600 | tf_op jit(solution)/shard_map/reduce_scatter | solution.py:72
  159.5 3.5 copy-start.7
  159.5 3.7 copy-start.12
  167.3 3.8 copy-start.19
  167.7 3.1 collective-permute-start.1
  175.2 6.1 copy-start.24
  175.2 6.1 copy-start.31
  181.3 5.1 copy-start.30
  186.4 5.1 copy-start.3
  186.4 5.1 copy-start.18
  205.7 57.0 %all-to-all-start.5 = ((bf16[2,512,1024]{2,1,0:T(8,128)(2,1)}), bf16[2,512,1024]{2,1,0:T(8,128)(2,1)}, u32[]{:S(2)}, u32[]{:S(2)}) async-start(bf16[2,512,1024]{2,1,0:T(8,128)(2,1)} %broadcast_in_dim.16), calls=%async_computation.5 | async-start | bytes 4194304 | tf_op jit(solution)/shard_map/all_to_all | solution.py:16
  262.7 34.6 %all-to-all-start.2 = ((bf16[2,512,512]{2,1,0:T(8,128)(2,1)}), bf16[2,512,512]{2,1,0:T(8,128)(2,1)S(1)}, u32[]{:S(2)}, u32[]{:S(2)}) async-start(bf16[2,512,512]{2,1,0:T(8,128)(2,1)} %bitcast.129), calls=%async_computation.2 | async-start | bytes 2097152 | tf_op jit(solution)/shard_map/all_to_all | solution.py:50
  298.7 18.8 %copy-start.8 = (f32[512,1024]{1,0:T(8,128)S(1)}, f32[512,1024]{1,0:T(8,128)}, u32[]{:S(2)}) copy-start(f32[512,1024]{1,0:T(8,128)} %get-tuple-element.88) | copy-start | bytes 6291460
  298.7 41.3 %all-to-all-start.6 = ((f32[64,1,3584]{2,1,0:T(1,128)}), f32[64,1,3584]{2,1,0:T(1,128)}, u32[]{:S(2)}, u32[]{:S(2)}) async-start(f32[64,1,3584]{2,1,0:T(1,128)} %broadcast_in_dim.17), calls=%async_computation.6 | async-start | bytes 1835008 | tf_op jit(solution)/shard_map/all_to_all | solution.py:16
  319.8 290.5 %copy-start.1 = (bf16[512,1024]{1,0:T(8,128)(2,1)S(1)}, bf16[512,1024]{1,0:T(8,128)(2,1)}, u32[]{:S(2)}) copy-start(bf16[512,1024]{1,0:T(8,128)(2,1)} %param.14) | copy-start | bytes 3145732
  (15 other events, 30.9 us)
Sparse Core Ops, SparseCore 0:
  199.5 405.9 reduce-scatter.1
where the time goes:
time: 619 us; the launch traced here: 617 us
  waiting for transfers between devices  398 us (64%)
  matrix products  66.5 us (11%)
  local copies, waits for them, and re-layouts  52.1 us (8%)
  starting transfers between devices  48.1 us (8%)
  other arithmetic  37.8 us (6%)
  between operations  14.6 us (2%)
    reduce_scatter x1, waiting for transfers between devices, side_by_side(): whole = lax.psum_scatter(both, axis, scatter_dimension=dim, tiled=True)  263 us
    all_to_all x6, waiting for transfers between devices, sent_to_all(): lax.all_to_all(jnp.broadcast_to(array[None], (length, *array.shape)), axi...  114 us
    all_to_all x6, starting transfers between devices, sent_to_all(): lax.all_to_all(jnp.broadcast_to(array[None], (length, *array.shape)), axi...  41.4 us
    all_to_all x1, waiting for transfers between devices, sent_and_summed(): lax.all_to_all(blocks, axis, split_axis=0, concat_axis=0, tiled=True)  19.6 us
    unnamed x77, local copies, waits for them, and re-layouts  14.9 us
  transfers between devices with their start and end apart: 10, of which 9 were waited for; matrix products, arithmetic and copies ran while one was open for 9% of the time, Pallas kernels for 0%

commit v1 on v0

v1 whole, which is shorter than its diff:
```python
import jax
import jax.numpy as jnp
from jax import lax
from jax.experimental import pallas as pl
from jax.experimental.pallas import tpu as pltpu
from jax.sharding import PartitionSpec as P

SEQS = 2
NORM_EPS = 1e-05
MESH = pl.DeviceIdType.MESH
F32 = jnp.float32
BF16 = jnp.bfloat16
VMEM_LIMIT = 66_000_000

ROWS = 512
D = 1024
HALF = 512
FFH = 2304
WF = 1152
WT = 1024
KEYS = ("c", "e1p", "e1m", "e2p", "e2m", "f1p", "f1m", "f2p", "f2m", "h")


def nt(a, b):
    return lax.dot_general(a, b, (((1,), (1,)), ((), ())), preferred_element_type=F32)


def nn(a, b):
    return jnp.dot(a, b, preferred_element_type=F32)


def mod(a, n):
    return lax.rem(a, n)


def neighbours():
    s = lax.axis_index("seq")
    sh = lax.axis_index("shard")
    y, zh, x, c = s // 16, mod(s // 8, 2), mod(s // 2, 4), mod(s, 2)

    def at(y_, zh_, x_, c_):
        return (((y_ * 2 + zh_) * 4 + x_) * 2 + c_, sh)

    to = {
        "z": (s, 1 - sh),
        "c": at(y, zh, x, 1 - c),
        "xp": at(y, zh, mod(x + 1, 4), c),
        "xm": at(y, zh, mod(x + 3, 4), c),
        "x2": at(y, zh, mod(x + 2, 4), c),
        "yp": at(mod(y + 1, 4), zh, x, c),
        "ym": at(mod(y + 3, 4), zh, x, c),
        "y2": at(mod(y + 2, 4), zh, x, c),
        "zh": at(y, 1 - zh, x, c),
        "nx": (mod(s + 1, 64), sh),
        "pv": (mod(s + 63, 64), sh),
    }
    return s, sh, (y, zh, x, c), to


def greet(to, names):
    barrier = pltpu.get_barrier_semaphore()
    for name in names:
        pl.semaphore_signal(barrier, inc=1, device_id=to[name], device_id_type=MESH)
    pl.semaphore_wait(barrier, len(names))


def send(src, dst, sems, rems, device):
    return pltpu.make_async_remote_copy(
        src_ref=src,
        dst_ref=dst,
        send_sem=sems,
        recv_sem=rems,
        device_id=device,
        device_id_type=MESH,
    )


def added(dst, *others):
    blocks = dst.shape[0]

    def step(i, _):
        total = dst[i].astype(F32)
        for o in others:
            total = total + o[i].astype(F32)
        dst[i] = total.astype(BF16)
        return 0

    lax.fori_loop(0, blocks, step, 0)


class Half:
    def __init__(self, first, to, s_ref, bufs, sems, rems):
        self.first, self.to, self.s, self.b = first, to, s_ref, bufs
        self.sems, self.rems = sems, rems
        self.ups = ("xp", "xm", "yp", "ym") if first == 0 else ("yp", "ym", "xp", "xm")
        self.sent = []
        self.made = {}

    def view(self, i, j):
        i, j = (i, j) if self.first == 0 else (j, i)
        i = slice(None) if i is None else (pl.ds(*i) if isinstance(i, tuple) else i)
        j = slice(None) if j is None else (pl.ds(*j) if isinstance(j, tuple) else j)
        return self.s.at[i, j]

    def go(self, key, src, dst, name):
        k = KEYS.index(key)
        copy = send(src, dst, self.sems.at[k], self.rems.at[k], self.to[name])
        copy.start()
        self.made[key] = copy

    def arrived(self, *keys):
        for k in keys:
            self.made[k].wait_recv()

    def core(self, g_ref):
        self.go("c", g_ref, self.s, "c")

    def e1(self):
        self.go("e1p", self.view(2, (0, 2)), self.b["e1p"], self.ups[0])
        self.go("e1m", self.view(2, (2, 2)), self.b["e1m"], self.ups[1])

    def e2(self):
        self.arrived("e1p", "e1m")
        added(self.view(1, (0, 2)), self.b["e1p"])
        self.go("e2p", self.view(1, None), self.b["e2p"], self.ups[0])
        added(self.view(3, (2, 2)), self.b["e1m"])
        self.go("e2m", self.view(3, None), self.b["e2m"], self.ups[1])

    def f1(self):
        self.arrived("e2p", "e2m")
        added(self.view(0, None), self.b["e2p"], self.b["e2m"])
        t = self.view(0, 2)
        self.go("f1p", t.at[pl.ds(0, 16)], self.b["f1p"], self.ups[2])
        self.go("f1m", t.at[pl.ds(16, 16)], self.b["f1m"], self.ups[3])

    def f2(self):
        self.arrived("f1p", "f1m")
        t1, t3 = self.view(0, 1), self.view(0, 3)
        t1[0:16, :] = (t1[0:16, :].astype(F32) + self.b["f1p"][...].astype(F32)).astype(BF16)
        self.go("f2p", t1, self.b["f2p"], self.ups[2])
        t3[16:32, :] = (t3[16:32, :].astype(F32) + self.b["f1m"][...].astype(F32)).astype(BF16)
        self.go("f2m", t3, self.b["f2m"], self.ups[3])

    def hop(self):
        self.arrived("f2p", "f2m")
        t = self.view(0, 0)
        t[...] = (
            t[...].astype(F32) + self.b["f2p"][...].astype(F32) + self.b["f2m"][...].astype(F32)
        ).astype(BF16)
        self.go("h", t.at[pl.ds(16, 16)], self.b["h"], "zh")

    def result(self):
        self.arrived("h")
        return self.view(0, 0)[0:16, :].astype(F32) + self.b["h"][...].astype(F32)

    def finish(self):
        for k in KEYS:
            if k != "c":
                self.made[k].wait_send()


def half_bufs(n, w):
    return [
        pltpu.VMEM((n, 4, 4, 32, w), BF16),
        pltpu.VMEM((n, 2, 2, 32, w), BF16),
        pltpu.VMEM((n, 2, 4, 32, w), BF16),
        pltpu.VMEM((n, 2, 16, w), BF16),
        pltpu.VMEM((n, 2, 32, w), BF16),
        pltpu.VMEM((n, 16, w), BF16),
    ]


def halves(n, to, refs, sems, rems, base):
    s, e1, e2, f1, f2, h = refs
    out = []
    for i in range(n):
        bufs = {
            "e1p": e1.at[i, 0],
            "e1m": e1.at[i, 1],
            "e2p": e2.at[i, 0],
            "e2m": e2.at[i, 1],
            "f1p": f1.at[i, 0],
            "f1m": f1.at[i, 1],
            "f2p": f2.at[i, 0],
            "f2m": f2.at[i, 1],
            "h": h.at[i],
        }
        out.append(Half(i % 2, to, s.at[i], bufs, sems.at[base + i], rems.at[base + i]))
    return out


def tiles(n, body):
    lax.fori_loop(0, n, lambda i, _: (body(i), 0)[1], 0)


def mult(i, n):
    return pl.multiple_of(i * n, n)


def turned(perm, at_ref, a_ref):
    def step(t):
        rows = pl.ds(mult(t, 256), 256)
        at_ref[rows, :] = nt(perm[rows, :], a_ref[...]).astype(BF16)

    tiles(4, step)


def order_matrix(perm, place):
    y, zh, x, c = place
    k = lax.broadcasted_iota(jnp.int32, (1, D), 1)
    k16 = k >> 4
    crel = ((k16 & 1) - c) & 1
    xrel = (((k16 >> 1) & 3) - x) & 3
    zrel = (((k16 >> 3) & 1) - zh) & 1
    yrel = ((k16 >> 4) - y) & 3
    pos = (((crel * 4 + xrel) * 4 + yrel) * 2 + zrel) * 16 + (k & 15)

    def step(t):
        r = lax.broadcasted_iota(jnp.int32, (128, D), 0) + t * 128
        perm[pl.ds(mult(t, 128), 128), :] = jnp.where(r == pos, 1.0, 0.0).astype(BF16)

    tiles(8, step)


def backward_kernel(
    da_in, db_in, u_in, wg_in, wu_in, hn_in, cot_in, x_in, h_in, p_in, conv_in, y_in,
    wout_in, win_in, halo, cw, g1, g2,
    tg, gate_o, up_o, down_o, out_o, in_o, vec_o,
    da, db, u, wbuf, cot, xv, hv, p, conv, yv, wout, dm, perm, dsend, drecv, dh, bx, dce, halo_in,
    dp, xs, xr, own, rd, rds, rdr, r1v, acc, gbuf, vs, vx, vy,
    s_f, e1_f, e2_f, f1_f, f2_f, h_f, s_t, e1_t, e2_t, f1_t, f2_t, h_t,
    lsem, rs_s, rs_r, ms, mr,
):
    s, sh, place, to = neighbours()
    loads = []

    def load(src, dst):
        copy = pltpu.make_async_copy(src, dst, lsem.at[len(loads)])
        copy.start()
        loads.append(copy)
        return copy

    l_da = load(da_in, da)
    l_wg = load(wg_in, wbuf.at[0])
    l_db = load(db_in, db)
    l_wu = load(wu_in, wbuf.at[1])
    l_hn = load(hn_in, dm)
    l_u = load(u_in, u)
    l_cot = load(cot_in, cot)
    l_h = load(h_in, hv)
    l_x = load(x_in, xv)
    l_conv = load(conv_in, conv)
    l_p = load(p_in, p)
    l_wout = load(wout_in, wout)
    l_y = load(y_in, yv)
    greet(to, ("z", "c", "xp", "xm", "x2", "yp", "ym", "y2", "zh", "nx", "pv"))
    order_matrix(perm, place)

    made = []

    def go(src, dst, name):
        k = len(made)
        copy = send(src, dst, ms.at[k], mr.at[k], to[name])
        copy.start()
        made.append(copy)
        return copy

    for l in (l_da, l_wg, l_db, l_wu):
        l.wait()
    z_dhn = []
    for r in range(2):
        rows = pl.ds(256 * r, 256)

        def step(n, rows=rows):
            cols = pl.ds(mult(n, 256), 256)
            t = nt(da[rows, :], wbuf[0, cols, :]) + nt(db[rows, :], wbuf[1, cols, :])
            dsend[rows, cols] = t.astype(BF16)

        tiles(4, step)
        z_dhn.append(go(dsend.at[rows], drecv.at[rows], "z"))

    win = wbuf.at[0, :, pl.ds(0, 3 * HALF)]
    l_win = load(win_in, win)
    hnt = wbuf.at[1, :, pl.ds(0, 512)]
    cott = wbuf.at[1, :, pl.ds(512, 512)]
    xnt = wbuf.at[1, :, pl.ds(1024, 512)]
    dmt = wbuf.at[1, :, pl.ds(1536, 512)]
    l_hn.wait()
    turned(perm, hnt, dm)
    l_cot.wait()
    turned(perm, cott, cot)
    l_u.wait()

    ffn = halves(6, to, (s_f, e1_f, e2_f, f1_f, f2_f, h_f), rs_s, rs_r, 0)
    tail = halves(2, to, (s_t, e1_t, e2_t, f1_t, f2_t, h_t), rs_s, rs_r, 6)
    ffn_parts = [(hnt, da), (hnt, db), (cott, u)]

    def ffn_send(i):
        at, b = ffn_parts[i // 2]
        slot = i % 3
        if i >= 3:
            ffn[i - 3].made["c"].wait_send()

        def step(n):
            t = nn(at[pl.ds(512, 512), :], b[:, pl.ds(pl.multiple_of((i % 2) * WF + n * 384, 128), 384)])
            gbuf[slot, :, :, :, pl.ds(mult(n, 384), 384)] = t.astype(BF16).reshape(4, 4, 32, 384)

        tiles(3, step)
        ffn[i].core(gbuf.at[slot])

    def ffn_keep(i):
        at, b = ffn_parts[i // 2]
        ffn[i].arrived("c")

        def step(n):
            t = nn(at[pl.ds(0, 512), :], b[:, pl.ds(pl.multiple_of((i % 2) * WF + n * 384, 128), 384)])
            cols = pl.ds(mult(n, 384), 384)
            t = t.reshape(4, 4, 32, 384) + s_f[i, :, :, :, cols].astype(F32)
            s_f[i, :, :, :, cols] = t.astype(BF16)

        tiles(3, step)
        ffn[i].e1()

    for i in range(3):
        ffn_send(i)
    l_x.wait()

    def xstep(t):
        rows = pl.ds(mult(t, 32), 32)
        xf = xv[rows, :].astype(F32)
        r1 = lax.rsqrt(jnp.mean(xf * xf, axis=-1, keepdims=True) + NORM_EPS)
        r1v[rows, :] = jnp.broadcast_to(r1, (32, 128))
        dm[rows, :] = (xf * r1 * g1[...]).astype(BF16)

    tiles(ROWS // 32, xstep)
    turned(perm, xnt, dm)
    for i in range(6):
        ffn_keep(i)
        if i + 3 < 6:
            ffn_send(i + 3)
    for i in range(2):
        ffn[i].e2()

    for l in (l_h, l_wout, l_conv, l_p):
        l.wait()
    acc[...] = jnp.zeros_like(acc)

    def bstep(t):
        rows = pl.ds(mult(t, 64), 64)
        bx[pl.ds(pl.multiple_of(t * 64 + 8, 8), 64), :] = p[rows, 0:512] * p[rows, 1024:1536]

    tiles(8, bstep)
    bx[0:8, :] = halo[...]

    def mixer(r):
        z_dhn[r].wait_recv()

        def step(t):
            rows = pl.ds(pl.multiple_of(r * 256 + t * 32, 32), 32)
            hf = hv[rows, :]
            r2 = lax.rsqrt(jnp.mean(hf * hf, axis=-1, keepdims=True) + NORM_EPS)
            dhn = dsend[rows, :].astype(F32) + drecv[rows, :].astype(F32)
            acc[0:8, :] += (dhn * hf * r2).reshape(4, 8, D).sum(axis=0)
            scaled = dhn * g2[...]
            dot = jnp.mean(scaled * hf, axis=-1, keepdims=True)
            d = cot[rows, :].astype(F32) + r2 * scaled - hf * (r2 * r2 * r2 * dot)
            dm[rows, :] = d.astype(BF16)
            dh[rows, :] = jnp.where(sh == 0, d[:, 0:512], d[:, 512:1024])

        tiles(8, step)
        for n in range(2):
            cols = pl.ds(256 * n, 256)
            rows = pl.ds(256 * r, 256)
            dy = nt(dm[rows, :], wout[cols, :])
            own[rows, cols] = dy
            dce[rows, cols] = dy * p[rows, pl.ds(512 + 256 * n, 256)]

    mixer(0)
    back = go(dce.at[pl.ds(0, 8)], halo_in, "pv")
    for i in range(2, 6):
        ffn[i].e2()
    mixer(1)
    back.wait_recv()
    last = mod(s, 32) == 31
    dce[512:520, :] = jnp.where(last, 0.0, halo_in[...])

    def dstep(t):
        rows = pl.ds(mult(t, 64), 64)
        ext = pl.ds(mult(t, 64), 72)
        dc = dce[ext, :]
        b = bx[ext, :]
        d0 = dc[0:64]
        acc[8:16, 0:512] += (d0 * b[6:70]).reshape(8, 8, 512).sum(axis=0)
        acc[16:24, 0:512] += (d0 * b[7:71]).reshape(8, 8, 512).sum(axis=0)
        acc[24:32, 0:512] += (d0 * b[8:72]).reshape(8, 8, 512).sum(axis=0)
        dbx = cw[2:3, :] * d0 + cw[1:2, :] * dc[1:65] + cw[0:1, :] * dc[2:66]
        dp[rows, 0:512] = (dbx * p[rows, 1024:1536]).astype(BF16)
        dp[rows, 512:1024] = (own[rows, :] * conv[rows, :]).astype(BF16)
        dp[rows, 1024:1536] = (dbx * p[rows, 0:512]).astype(BF16)

    tiles(8, dstep)

    l_win.wait()
    rd[...] = jnp.zeros_like(rd)
    acc[32:40, :] = jnp.zeros((8, D), F32)

    def dxn(half, dst):
        for n in range(2):
            wr = pl.ds(pl.multiple_of(half * 512 + n * 256, 256), 256)

            def step(r, n=n, wr=wr):
                rows = pl.ds(mult(r, 256), 256)
                t = nt(dp[rows, :], win[wr, :])
                xt = xv[rows, wr].astype(F32)
                tx = t * xt
                rd[rows, :] += jnp.broadcast_to(
                    jnp.sum(tx * g1[:, wr], axis=-1, keepdims=True), (256, 128)
                )
                acc[32:40, wr] += (tx * r1v[rows, 0:1]).reshape(32, 8, 256).sum(axis=0)
                dst[rows, pl.ds(256 * n, 256)] = t.astype(dst.dtype)

            tiles(2, step)

    dxn(1 - sh, xs)
    z_dxn = go(xs, xr, "z")
    dxn(sh, own)
    hi = rd[...].astype(BF16)
    lo = (rd[...] - hi.astype(F32)).astype(BF16)
    lane = lax.broadcasted_iota(jnp.int32, (ROWS, 128), 1)
    rds[...] = jnp.where(lane < 64, hi.astype(F32), lo.astype(F32)).astype(BF16)
    z_rd = go(rds, rdr, "z")

    row = lax.broadcasted_iota(jnp.int32, (8, D), 0)

    def total(lo_, lanes=D):
        t = jnp.sum(acc[lo_ : lo_ + 8, :], axis=0, keepdims=True)
        return jnp.broadcast_to(t, (8, D))

    v = jnp.where(row == 0, total(32), 0.0)
    v = jnp.where(row == 1, 0.5 * total(0), v)
    v = jnp.where(row == 2, total(8), v)
    v = jnp.where(row == 3, total(16), v)
    v = jnp.where(row == 4, total(24), v)
    vs[0] = v
    v_z = go(vs.at[0], vs.at[5], "z")

    l_y.wait()
    turned(perm, dmt, dm)

    def tail_gemm(i, lo_, store):
        rows = pl.ds(lo_, 512)
        store(0, nn(dmt[rows, :], yv[:, pl.ds(i * 256, 256)]))

        def step(n):
            store(n + 1, nn(xnt[rows, :], dp[:, pl.ds(pl.multiple_of(i * 768 + n * 256, 256), 256)]))

        tiles(3, step)

    def tail_send(i):
        ffn[3 + i].made["c"].wait_send()

        def store(n, t):
            cols = pl.ds(mult(n, 256), 256)
            gbuf[i, :, :, :, cols] = t.astype(BF16).reshape(4, 4, 32, 256)

        tail_gemm(i, 512, store)
        tail[i].core(gbuf.at[i, :, :, :, pl.ds(0, WT)])

    def tail_keep(i):
        tail[i].arrived("c")

        def store(n, t):
            cols = pl.ds(mult(n, 256), 256)
            t = t.reshape(4, 4, 32, 256) + s_t[i, :, :, :, cols].astype(F32)
            s_t[i, :, :, :, cols] = t.astype(BF16)

        tail_gemm(i, 0, store)
        tail[i].e1()

    tail_send(0)
    tail_send(1)
    for i in range(3):
        ffn[i].f1()
    tail_keep(0)
    tail_keep(1)
    v_z.wait_recv()
    vs[1] = vs[0] + jnp.where(row < 2, vs[5], 0.0)
    v_c = go(vs.at[1], vs.at[6], "c")
    for i in range(3, 6):
        ffn[i].f1()
    for i in range(2):
        tail[i].e2()
    for i in range(3):
        ffn[i].f2()
    v_c.wait_recv()
    vs[2] = vs[1] + vs[6]
    y, zh, x, c = place
    vx[x] = vs[2]
    v_x = [go(vs.at[2], vx.at[x], n) for n in ("xp", "xm", "x2")]
    for i in range(3, 6):
        ffn[i].f2()

    z_dxn.wait_recv()
    z_rd.wait_recv()

    def tstep(t):
        rows = pl.ds(mult(t, 64), 64)
        cols = pl.ds(mult(sh, 512), 512)
        r1 = r1v[rows, 0:1]
        d = own[rows, :] + xr[rows, :].astype(F32)
        q = rdr[rows, :].astype(F32)
        mean = (rd[rows, 0:1] + q[:, 0:1] + q[:, 64:65]) * (1.0 / D)
        xo = xv[rows, cols].astype(F32)
        tg[rows, :] = dh[rows, :] + r1 * (d * g1[:, cols]) - xo * (r1 * r1 * r1 * mean)

    tiles(8, tstep)

    for i in range(2):
        tail[i].f1()
    for w in v_x:
        w.wait_recv()
    vs[3] = (vx[0] + vx[1]) + (vx[2] + vx[3])
    vy[y] = vs[3]
    v_y = [go(vs.at[3], vy.at[y], n) for n in ("yp", "ym", "y2")]
    for i in range(6):
        ffn[i].hop()
    for i in range(2):
        tail[i].f2()
    for w in v_y:
        w.wait_recv()
    vs[4] = (vy[0] + vy[1]) + (vy[2] + vy[3])
    v_h = go(vs.at[4], vs.at[7], "zh")
    for i, o in enumerate((gate_o, up_o, down_o)):
        o[:, 0:WF] = ffn[2 * i].result()
        o[:, WF : 2 * WF] = ffn[2 * i + 1].result()
    for i in range(2):
        tail[i].hop()
    for i in range(2):
        t = tail[i].result()
        out_o[:, 256 * i : 256 * i + 256] = t[:, 0:256]
        in_o[:, 768 * i : 768 * i + 768] = t[:, 256:1024]
    v_h.wait_recv()
    vec_o[...] = vs[4] + vs[7]
    for q in made:
        q.wait_send()
    for q in ffn + tail:
        q.finish()
    for i in (5,):
        ffn[i].made["c"].wait_send()
    for q in tail:
        q.made["c"].wait_send()


def backward(da, db, u, wg, wu, hn, cot, x, h, p, conv, y, wout, win, halo, cw, g1, g2):
    hbm = pl.BlockSpec(memory_space=pl.ANY)
    vm = pl.BlockSpec(memory_space=pltpu.VMEM)
    sds = jax.ShapeDtypeStruct
    scratch = [
        pltpu.VMEM((ROWS, FFH), BF16),
        pltpu.VMEM((ROWS, FFH), BF16),
        pltpu.VMEM((ROWS, FFH), BF16),
        pltpu.VMEM((2, D, FFH), BF16),
        pltpu.VMEM((ROWS, D), BF16),
        pltpu.VMEM((ROWS, D), BF16),
        pltpu.VMEM((ROWS, D), F32),
        pltpu.VMEM((ROWS, 3 * HALF), F32),
        pltpu.VMEM((ROWS, HALF), F32),
        pltpu.VMEM((ROWS, HALF), BF16),
        pltpu.VMEM((HALF, D), BF16),
        pltpu.VMEM((ROWS, D), BF16),
        pltpu.VMEM((D, D), BF16),
        pltpu.VMEM((ROWS, D), BF16),
        pltpu.VMEM((ROWS, D), BF16),
        pltpu.VMEM((ROWS, HALF), F32),
        pltpu.VMEM((ROWS + 8, HALF), F32),
        pltpu.VMEM((ROWS + 8, HALF), F32),
        pltpu.VMEM((8, HALF), F32),
        pltpu.VMEM((ROWS, 3 * HALF), BF16),
        pltpu.VMEM((ROWS, HALF), BF16),
        pltpu.VMEM((ROWS, HALF), BF16),
        pltpu.VMEM((ROWS, HALF), F32),
        pltpu.VMEM((ROWS, 128), F32),
        pltpu.VMEM((ROWS, 128), BF16),
        pltpu.VMEM((ROWS, 128), BF16),
        pltpu.VMEM((ROWS, 128), F32),
        pltpu.VMEM((40, D), F32),
        pltpu.VMEM((3, 4, 4, 32, WF), BF16),
        pltpu.VMEM((8, 8, D), F32),
        pltpu.VMEM((4, 8, D), F32),
        pltpu.VMEM((4, 8, D), F32),
        *half_bufs(6, WF),
        *half_bufs(2, WT),
        pltpu.SemaphoreType.DMA((16,)),
        pltpu.SemaphoreType.DMA((8, len(KEYS))),
        pltpu.SemaphoreType.DMA((8, len(KEYS))),
        pltpu.SemaphoreType.DMA((16,)),
        pltpu.SemaphoreType.DMA((16,)),
    ]
    return pl.pallas_call(
        backward_kernel,
        out_shape=(
            sds((ROWS, HALF), F32),
            sds((16, FFH), F32),
            sds((16, FFH), F32),
            sds((16, FFH), F32),
            sds((16, HALF), F32),
            sds((16, 3 * HALF), F32),
            sds((8, D), F32),
        ),
        in_specs=[hbm] * 14 + [vm] * 4,
        out_specs=(vm,) * 7,
        scratch_shapes=scratch,
        compiler_params=pltpu.CompilerParams(
            collective_id=1, has_side_effects=True, vmem_limit_bytes=VMEM_LIMIT
        ),
        cost_estimate=pl.CostEstimate(
            flops=20_000_000_000, bytes_accessed=40_000_000, transcendentals=0
        ),
        name="backward",
    )(da, db, u, wg, wu, hn, cot, x, h, p, conv, y, wout, win, halo, cw, g1, g2)


def shifted(block, axis, distance):
    devices = range(lax.axis_size(axis))
    route = [(i - distance, i) for i in devices if i - distance in devices]
    return lax.ppermute(block, axis, route)


def swapped(block):
    return lax.ppermute(block, "shard", [(0, 1), (1, 0)])


def joined(own, other):
    first = lax.axis_index("shard") == 0
    return jnp.concatenate([jnp.where(first, own, other), jnp.where(first, other, own)], axis=1)


def body(
    tokens, norm_gain, in_weight, conv_weight, out_weight, ffn_gain, gate_weight, up_weight,
    down_weight, cotangent,
):
    shard_start = lax.axis_index("shard") * HALF
    other = swapped(tokens)
    cot_mine, other = lax.optimization_barrier((cotangent, other))
    cot_other = swapped(cot_mine)
    x = joined(tokens, other)
    x_full = x.astype(F32)
    gain_one = norm_gain.astype(F32)[None]
    gain_two = ffn_gain.astype(F32)[None]
    inv_one = lax.rsqrt(jnp.mean(x_full * x_full, axis=-1, keepdims=True) + NORM_EPS)
    normed_in = (x_full * inv_one * gain_one).astype(BF16)
    w_in = in_weight.reshape(D, -1)
    projected = jnp.dot(normed_in, w_in, preferred_element_type=F32)
    b_gate, c_gate, x_gate = jnp.split(projected, 3, axis=1)
    gated = b_gate * x_gate
    per_seq = lax.axis_size("seq") // SEQS
    seq_start = lax.axis_index("seq") % per_seq == 0
    before = jnp.where(seq_start, 0.0, shifted(gated[-8:], "seq", 1))
    extended = jnp.concatenate([before[-2:], gated], axis=0)
    taps = conv_weight.astype(F32)
    conv = taps[0] * extended[:-2] + taps[1] * extended[1:-1] + taps[2] * extended[2:]
    mixed = (c_gate * conv).astype(BF16)
    m_own = jnp.dot(mixed, out_weight, preferred_element_type=F32).astype(BF16)
    stream = x_full + m_own.astype(F32) + swapped(m_own).astype(F32)
    stream_own = lax.dynamic_slice_in_dim(stream, shard_start, HALF, 1)
    inv_two = lax.rsqrt(jnp.mean(stream * stream, axis=-1, keepdims=True) + NORM_EPS)
    normed_mid = (stream * inv_two * gain_two).astype(BF16)
    a = jnp.dot(normed_mid, gate_weight, preferred_element_type=F32)
    b = jnp.dot(normed_mid, up_weight, preferred_element_type=F32)
    sig = jax.nn.sigmoid(a)
    silu = a * sig
    hidden = (silu * b).astype(BF16)
    terms = jnp.dot(hidden, down_weight, preferred_element_type=F32).astype(BF16)
    terms_own = lax.dynamic_slice_in_dim(terms, shard_start, HALF, 1)
    terms_other = lax.dynamic_slice_in_dim(terms, HALF - shard_start, HALF, 1)
    arrived = swapped(terms_other)
    block_out = (stream_own + terms_own.astype(F32) + arrived.astype(F32)).astype(BF16)
    cot = joined(cotangent, cot_other)
    du = jnp.einsum("td,fd->tf", cot, down_weight, preferred_element_type=F32)
    da = (du * b * sig * (1.0 + a * (1.0 - sig))).astype(BF16)
    db = (du * silu).astype(BF16)
    tg, gate_g, up_g, down_g, out_g, in_g, vec = backward(
        da, db, hidden, gate_weight, up_weight, normed_mid, cot, x, stream, projected, conv, mixed,
        out_weight, w_in, before, taps, gain_one, gain_two,
    )
    return (
        block_out,
        tg,
        vec[0],
        in_g.reshape(16, 3, HALF),
        vec[2:5, :HALF],
        out_g.T,
        vec[1],
        gate_g,
        up_g,
        down_g.T,
    )


def solution(mesh):
    return jax.shard_map(
        body,
        mesh=mesh,
        in_specs=(
            P("seq", "shard"),
            P(),
            P(None, None, "shard"),
            P(None, "shard"),
            P("shard", None),
            P(),
            P(None, "shard"),
            P(None, "shard"),
            P("shard", None),
            P("seq", "shard"),
        ),
        out_specs=(
            P("seq", "shard"),
            P("seq", "shard"),
            P(),
            P("seq", None, "shard"),
            P(None, "shard"),
            P("shard", "seq"),
            P(),
            P("seq", "shard"),
            P("seq", "shard"),
            P("shard", "seq"),
        ),
        check_vma=False,
    )
```

time: 619 us -> 202 us (0.33)
  waiting for transfers between devices: 398 us -> 38 us
  Pallas kernels: 0 us -> 97.6 us
  matrix products: 66.5 us -> 23 us
  starting transfers between devices: 48.1 us -> 8.09 us
  local copies, waits for them, and re-layouts: 52.1 us -> 18 us
  other arithmetic: 37.8 us -> 16.1 us
  between operations: 14.6 us -> 0.97 us
    reduce_scatter x1 -> x0, waiting for transfers between devices: 263 us -> none  [side_by_side(): whole = lax.psum_scatter(both, axis, scatter_dimension=dim, tiled=True)]
    all_to_all x7 -> x0, waiting for transfers between devices: 133 us -> none  [the longest x6 114 us: sent_to_all(): lax.all_to_all(jnp.broadcast_to(array[None], (length, *array.shape)), axi...]
    pallas_call x0 -> x1, Pallas kernels: none -> 97.6 us  [backward(): pl.pallas_call(backward_kernel, out_shape=(sds((ROWS, HALF), F32), sds((1...]
    all_to_all x7 -> x0, starting transfers between devices: 45.2 us -> none  [the longest x6 41.4 us: sent_to_all(): lax.all_to_all(jnp.broadcast_to(array[None], (length, *array.shape)), axi...]
    dot_general x15 -> x6, matrix products: 66.5 us -> 23 us  [the longest x1 8.25 us: body(): du = jnp.einsum('td,fd->tf', cot, down_weight, preferred_element_type=F32)]
    ppermute x0 -> x4, waiting for transfers between devices: none -> 37.2 us  [swapped(): return lax.ppermute(block, 'shard', [(0, 1), (1, 0)])]
    reduce_sum x9 -> x1, other arithmetic: 22.7 us -> 2.09 us  [body(): jnp.mean(stream * stream, axis=-1, keepdims=True) + NORM_EPS]
    broadcast_in_dim x6 -> x0, local copies, waits for them, and re-layouts: 10.7 us -> none  [sent_to_all(): jnp.broadcast_to(array[None], (length, *array.shape))]
  transfers between devices with their start and end apart: 10 -> 5, of which waited for: 9 -> 4; matrix products, arithmetic and copies ran while one was open for 9% -> 7% of each run, Pallas kernels for 0% -> 48%
where the time goes in v1:
time: 202 us
  Pallas kernels  97.6 us (48%)
  waiting for transfers between devices  38 us (19%)
  matrix products  23 us (11%)
  local copies, waits for them, and re-layouts  18 us (9%)
  other arithmetic  16.1 us (8%)
  starting transfers between devices  8.09 us (4%)
    pallas_call x1, Pallas kernels, backward(): pl.pallas_call(backward_kernel, out_shape=(sds((ROWS, HALF), F32), sds((1...  97.6 us
    ppermute x4, waiting for transfers between devices, swapped(): return lax.ppermute(block, 'shard', [(0, 1), (1, 0)])  37.2 us
    unnamed x68, local copies, waits for them, and re-layouts  10.6 us
    dot_general x1, matrix products, body(): du = jnp.einsum('td,fd->tf', cot, down_weight, preferred_element_type=F32)  8.25 us
    ppermute x4, starting transfers between devices, swapped(): return lax.ppermute(block, 'shard', [(0, 1), (1, 0)])  6.81 us
    dot_general x1, matrix products, body(): a = jnp.dot(normed_mid, gate_weight, preferred_element_type=F32)  4.27 us
    dot_general x1, matrix products, body(): b = jnp.dot(normed_mid, up_weight, preferred_element_type=F32)  4.27 us
  transfers between devices with their start and end apart: 5, of which 4 were waited for; matrix products, arithmetic and copies ran while one was open for 7% of the time, Pallas kernels for 48%

profile of v1, /device:TPU:0, one launch (start us, length us, event | category | flops | bytes accessed | tf_op | source)
XLA Modules:
  0.0 201.7 jit_solution(6504516788979215305)
XLA Ops:
  0.6 2.1 %collective-permute-start = (bf16[512,512]{1,0:T(8,128)(2,1)}, bf16[512,512]{1,0:T(8,128)(2,1)}, u32[]{:S(2)}, u32[]{:S(2)}) collective-permute-start(bf16[512,512]{1,0:T(8,128)(2,1)} %param.10), channel_id=1, source_target_pairs={{0,1},{1,0},{2,3},{3,2},{4,5},{5,4},{6,7},{7,6},{8,9},{9,8},{10,11... | collective-permute-start | bytes 1572872 | tf_op jit(solution)/shard_map/ppermute | solution.py:630
  2.7 12.2 %collective-permute-done = bf16[512,512]{1,0:T(8,128)(2,1)} collective-permute-done((bf16[512,512]{1,0:T(8,128)(2,1)}, bf16[512,512]{1,0:T(8,128)(2,1)}, u32[]{:S(2)}, u32[]{:S(2)}) %collective-permute-start) | collective-permute-done | bytes 524320 | tf_op jit(solution)/shard_map/ppermute | solution.py:630
  15.0 1.7 collective-permute-start.4
  16.7 3.2 %copy.22 = bf16[1024,3,512]{0,2,1:T(8,128)(2,1)S(1)} copy(bf16[1024,3,512]{2,0,1:T(8,128)(2,1)} %param.12) | data formatting | bytes 6291456 | tf_op args[2]
  19.9 8.4 %collective-permute-done.4 = bf16[512,512]{1,0:T(8,128)(2,1)} collective-permute-done((bf16[512,512]{1,0:T(8,128)(2,1)}, bf16[512,512]{1,0:T(8,128)(2,1)}, u32[]{:S(2)}, u32[]{:S(2)}) %collective-permute-start.4) | collective-permute-done | bytes 524320 | tf_op jit(solution)/shard_map/ppermute | solution.py:630
  28.4 2.7 %broadcast_select_fusion.1 = (bf16[512,512]{1,0:T(8,128)(2,1)}, bf16[512,512]{1,0:T(8,128)(2,1)}, bf16[512,512]{1,0:T(8,128)(2,1)S(1)}, bf16[512,512]{1,0:T(8,128)(2,1)S(1)}) fusion(bf16[512,512]{1,0:T(8,128)(2,1)} %param.19, bf16[512,512]{1,0:T(8,128)(2,1)} %collective-permute-done.4, pred[]{:T(512)S(6)} %eq.9, bf16[512,512]{1,0:T(8,128)(2,1)} %collective-permute-done, ...), kind=kLoop, calls=%fused_computation.34 | loop fusion | flops 1048576 | bytes 4194305 | tf_op jit(solution)/shard_map/jit(_where)/select_n | solution.py:635
  31.3 1.9 fusion.9.p_in
  33.5 1.2 copy-done.5
  35.3 1.3 collective-permute-start.1
  36.6 0.8 collective-permute-done.1
  37.4 3.9 %fusion.12 = (bf16[512,512]{1,0:T(8,128)(2,1)S(1)}, f32[512,512]{1,0:T(8,128)}) fusion(f32[512,1536]{1,0:T(8,128)} %copy-done.6, f32[512,512]{1,0:T(8,128)} %copy-done.5, f32[512]{0:T(512)S(1)} %bitcast.33, f32[2,512]{1,0:T(2,128)S(1)} %slice.42, f32[512]{0:T(512)S(1)} %bitcast.32, f32[512]{0:T(512)S(1)} %bitcast.31), kind=kLoop, calls=%fused_computation.27 | loop fusion | flops 2359296 | bytes 3680256 | tf_op jit(solution)/shard_map/convert_element_type | solution.py:662
  41.2 0.8 copy-done.12
  42.0 1.7 convolution_convert_fusion.1
  43.7 1.4 collective-permute-start.2
  45.2 3.0 %copy.23.win_in = bf16[1024,1536]{1,0:T(8,128)(2,1)} copy(bf16[1024,1536]{0,1:T(8,128)(2,1)S(1)} %bitcast.25) | data formatting | bytes 6291456 | tf_op jit(solution)/shard_map/reshape | solution.py:652
  48.8 2.4 %pad_maximum_fusion.1.x_in = bf16[512,1024]{1,0:T(8,128)(2,1)} fusion(bf16[512,512]{1,0:T(8,128)(2,1)} %copy-done.1, bf16[512,512]{1,0:T(8,128)(2,1)} %copy-done.3), kind=kLoop, calls=%fused_computation.28 | loop fusion | flops 2097152 | bytes 2097152 | tf_op jit(solution)/shard_map/concatenate | solution.py:635
  51.1 1.2 pad_maximum_fusion.2.cot_in
  52.4 16.5 %collective-permute-done.2 = bf16[512,1024]{1,0:T(8,128)(2,1)} collective-permute-done((bf16[512,1024]{1,0:T(8,128)(2,1)}, bf16[512,1024]{1,0:T(8,128)(2,1)}, u32[]{:S(2)}, u32[]{:S(2)}) %collective-permute-start.2) | collective-permute-done | bytes 1048608 | tf_op jit(solution)/shard_map/ppermute | solution.py:630
  68.9 2.1 %multiply_reduce_fusion = (f32[512]{0:T(512)S(1)}, f32[512,1024]{1,0:T(8,128)S(1)}) fusion(bf16[512,1024]{1,0:T(8,128)(2,1)} %collective-permute-done.2, bf16[512,1024]{1,0:T(8,128)(2,1)} %convolution_convert_fusion.1, bf16[512,512]{1,0:T(8,128)(2,1)S(1)} %copy-done.2, bf16[512,512]{1,0:T(8,128)(2,1)S(1)} %copy-done.4), kind=kLoop, calls=%fused_computation.13 | loop fusion | flops 5242368 | bytes 5244928 | tf_op jit(solution)/shard_map/reduce_sum | solution.py:666
  71.3 4.3 %fusion.20 = f32[512,2304]{1,0:T(8,128)} fusion(bf16[512,1024]{1,0:T(8,128)(2,1)S(1)} %multiply_convert_fusion.3.hn_in, bf16[1024,2304]{1,0:T(8,128)(2,1)S(1)} %bitcast.40), kind=kOutput, calls=%fused_computation.45 | convolution fusion | flops 2415919104 | bytes 10485760 | tf_op jit(solution)/shard_map/dot_general | solution.py:668
  75.8 4.3 %fusion.21 = f32[512,2304]{1,0:T(8,128)} fusion(bf16[512,1024]{1,0:T(8,128)(2,1)S(1)} %multiply_convert_fusion.3.hn_in, bf16[1024,2304]{1,0:T(8,128)(2,1)S(1)} %bitcast.42), kind=kOutput, calls=%fused_computation.46 | convolution fusion | flops 2415919104 | bytes 10485760 | tf_op jit(solution)/shard_map/dot_general | solution.py:669
  80.1 8.3 %multiply_convert_fusion = (bf16[512,2304]{1,0:T(8,128)(2,1)}, bf16[512,2304]{1,0:T(8,128)(2,1)}, bf16[512,2304]{1,0:T(8,128)(2,1)S(1)}) fusion(f32[512,2304]{1,0:T(8,128)} %fusion.20, f32[512,2304]{1,0:T(8,128)} %fusion.21, bf16[2304,1024]{1,0:T(8,128)(2,1)S(1)} %bitcast.38, bf16[512,512]{1,0:T(8,128)(2,1)S(1)} %copy-done.8, bf16[512,512]{1,0:T(8,128)(2,1)S(1)} %copy-done.7), kind=kOutput, calls=%fused_computation | convolution fusion | flops 2435710976 | bytes 22282240 | tf_op jit(solution)/shard_map/td,fd->tf/dot_general | solution.py:679
  88.4 2.6 %convolution_convert_fusion = bf16[512,1024]{1,0:T(8,128)(2,1)S(1)} fusion(bf16[512,2304]{1,0:T(8,128)(2,1)S(1)} %get-tuple-element.54.u_in, bf16[2304,1024]{1,0:T(8,128)(2,1)S(1)} %bitcast.38), kind=kOutput, calls=%fused_computation.14 | convolution fusion | flops 2416443392 | bytes 8126464 | tf_op jit(solution)/shard_map/dot_general | solution.py:673
  91.0 1.0 copy-done.11
  92.0 1.6 collective-permute-start.3
  93.6 97.6 %backward.1 = (f32[512,512]{1,0:T(8,128)}, f32[16,2304]{1,0:T(8,128)}, f32[16,2304]{1,0:T(8,128)}, f32[16,2304]{1,0:T(8,128)}, f32[16,512]{1,0:T(8,128)}, /*index=5*/f32[16,1536]{1,0:T(8,128)}, f32[8,1024]{1,0:T(8,128)}) custom-call(bf16[512,2304]{1,0:T(8,128)(2,1)} %get-tuple-element.53.da_in, bf16[512,2304]{1,0:T(8,128)(2,1)} %get-tuple-element.52.db_in, ...), custom_call_target="tpu_custom_call" | custom-call | flops 20000000000 | bytes 40000000 | tf_op jit(solution)/shard_map/backward/pallas_call | solution.py:599
  191.2 1.6 copy.27
  192.8 1.3 slice.38
  194.1 1.4 fusion.18
  195.6 2.6 %add_convert_fusion = bf16[512,512]{1,0:T(8,128)(2,1)} fusion(bf16[512,512]{1,0:T(8,128)(2,1)} %collective-permute-done.3, f32[512,1024]{1,0:T(8,128)} %copy-done, s32[]{:T(128)S(6)} %select_n.48, bf16[512,1024]{1,0:T(8,128)(2,1)} %copy-done.11), kind=kLoop, calls=%fused_computation.30 | loop fusion | flops 1310720 | bytes 2621444 | tf_op jit(solution)/shard_map/convert_element_type | solution.py:677
  198.2 1.0 copy.33
  199.8 0.7 copy.35
  (79 shorter events, 4.3 us)
Async XLA Ops:
  0.6 14.3 %collective-permute-start = (bf16[512,512]{1,0:T(8,128)(2,1)}, bf16[512,512]{1,0:T(8,128)(2,1)}, u32[]{:S(2)}, u32[]{:S(2)}) collective-permute-start(bf16[512,512]{1,0:T(8,128)(2,1)} %param.10), channel_id=1, source_target_pairs={{0,1},{1,0},{2,3},{3,2},{4,5},{5,4},{6,7},{7,6},{8,9},{9,8},{10,11... | collective-permute-start | bytes 1572872 | tf_op jit(solution)/shard_map/ppermute | solution.py:630
  15.0 13.4 %collective-permute-start.4 = (bf16[512,512]{1,0:T(8,128)(2,1)}, bf16[512,512]{1,0:T(8,128)(2,1)}, u32[]{:S(2)}, u32[]{:S(2)}) collective-permute-start(bf16[512,512]{1,0:T(8,128)(2,1)} %param.19), channel_id=1, source_target_pairs={{0,1},{1,0},{2,3},{3,2},{4,5},{5,4},{6,7},{7,6},{8,9},{9,8},{10,11... | collective-permute-start | bytes 1572872 | tf_op jit(solution)/shard_map/ppermute | solution.py:630
  16.7 3.2 %copy-start.21 = (bf16[1024]{0:T(1024)(128)(2,1)S(1)}, bf16[1024]{0:T(1024)(128)(2,1)}, u32[]{:S(2)}) copy-start(bf16[1024]{0:T(1024)(128)(2,1)} %param.11) | copy-start | bytes 6148
  19.9 11.4 %copy-start.20 = (f32[1024]{0:T(1024)}, f32[1024]{0:T(1024)S(1)}, u32[]{:S(2)}) copy-start(f32[1024]{0:T(1024)S(1)} %convert_element_type.52) | copy-start | bytes 12292
  31.0 2.2 %copy-start.1 = (bf16[512,512]{1,0:T(8,128)(2,1)}, bf16[512,512]{1,0:T(8,128)(2,1)S(1)}, u32[]{:S(2)}) copy-start(bf16[512,512]{1,0:T(8,128)(2,1)S(1)} %get-tuple-element.64) | copy-start | bytes 1572868
  31.0 2.2 %copy-start.3 = (bf16[512,512]{1,0:T(8,128)(2,1)}, bf16[512,512]{1,0:T(8,128)(2,1)S(1)}, u32[]{:S(2)}) copy-start(bf16[512,512]{1,0:T(8,128)(2,1)S(1)} %get-tuple-element.65) | copy-start | bytes 1572868
  33.3 3.3 %copy-start.17 = (bf16[3,512]{1,0:T(4,128)(2,1)S(1)}, bf16[3,512]{1,0:T(4,128)(2,1)}, u32[]{:S(2)}) copy-start(bf16[3,512]{1,0:T(4,128)(2,1)} %param.13) | copy-start | bytes 9220
  35.3 2.1 %collective-permute-start.1 = (f32[8,512]{1,0:T(8,128)S(1)}, f32[8,512]{1,0:T(8,128)S(1)}, u32[]{:S(2)}, u32[]{:S(2)}) collective-permute-start(f32[8,512]{1,0:T(8,128)S(1)} %slice.41), channel_id=1, source_target_pairs={{0,2},{2,4},{4,6},{6,8},{8,10},{10,12},{12,14},{14,16},{16,18},{18... | collective-permute-start | bytes 49160 | tf_op jit(solution)/shard_map/ppermute | solution.py:626
  36.6 5.5 %copy-start.23 = (bf16[512,1024]{1,0:T(8,128)(2,1)S(1)}, bf16[512,1024]{1,0:T(8,128)(2,1)}, u32[]{:S(2)}) copy-start(bf16[512,1024]{1,0:T(8,128)(2,1)} %wout_in.1) | copy-start | bytes 3145732
  37.4 6.4 %copy-start.18 = (f32[8,512]{1,0:T(8,128)}, f32[8,512]{1,0:T(8,128)S(1)}, u32[]{:S(2)}) copy-start(f32[8,512]{1,0:T(8,128)S(1)} %broadcast_select_fusion.4.halo) | copy-start | bytes 49156
  43.7 5.0 %copy-start.22 = (bf16[1024]{0:T(1024)(128)(2,1)S(1)}, bf16[1024]{0:T(1024)(128)(2,1)}, u32[]{:S(2)}) copy-start(bf16[1024]{0:T(1024)(128)(2,1)} %param.15) | copy-start | bytes 6148
  43.7 25.1 %collective-permute-start.2 = (bf16[512,1024]{1,0:T(8,128)(2,1)}, bf16[512,1024]{1,0:T(8,128)(2,1)}, u32[]{:S(2)}, u32[]{:S(2)}) collective-permute-start(bf16[512,1024]{1,0:T(8,128)(2,1)} %convolution_convert_fusion.1), channel_id=1, source_target_pairs={{0,1},{1,0},{2,3},{3,2},{4,5},{5,4},{6,7},{7,6},{8,9},{9,8},{10,11... | collective-permute-start | bytes 3145736 | tf_op jit(solution)/shard_map/ppermute | solution.py:630
  48.1 3.0 %copy-start.7 = (bf16[512,512]{1,0:T(8,128)(2,1)S(1)}, bf16[512,512]{1,0:T(8,128)(2,1)}, u32[]{:S(2)}) copy-start(bf16[512,512]{1,0:T(8,128)(2,1)} %get-tuple-element.55) | copy-start | bytes 1572868
  48.1 3.0 %copy-start.8 = (bf16[512,512]{1,0:T(8,128)(2,1)S(1)}, bf16[512,512]{1,0:T(8,128)(2,1)}, u32[]{:S(2)}) copy-start(bf16[512,512]{1,0:T(8,128)(2,1)} %get-tuple-element.56) | copy-start | bytes 1572868
  48.1 20.7 %copy-start.2 = (bf16[512,512]{1,0:T(8,128)(2,1)S(1)}, bf16[512,512]{1,0:T(8,128)(2,1)}, u32[]{:S(2)}) copy-start(bf16[512,512]{1,0:T(8,128)(2,1)} %copy-done.1) | copy-start | bytes 1572868
  48.1 20.7 %copy-start.4 = (bf16[512,512]{1,0:T(8,128)(2,1)S(1)}, bf16[512,512]{1,0:T(8,128)(2,1)}, u32[]{:S(2)}) copy-start(bf16[512,512]{1,0:T(8,128)(2,1)} %copy-done.3) | copy-start | bytes 1572868
  48.8 22.2 %copy-start.19 = (f32[1024]{0:T(1024)}, f32[1024]{0:T(1024)S(1)}, u32[]{:S(2)}) copy-start(f32[1024]{0:T(1024)S(1)} %convert_element_type.59) | copy-start | bytes 12292
  51.1 20.1 %slice-start.2 = ((s8[4718592]{0:T(1024)(128)(4,1)}), s8[4194304]{0:T(1024)(128)(4,1)S(1)}, s32[]{:S(2)}) async-start(s8[4718592]{0:T(1024)(128)(4,1)} %bitcast.39), calls=%async_computation.2 | async-start | bytes 8388608
  52.4 18.9 %slice-start.3 = ((s8[4718592]{0:T(1024)(128)(4,1)}), s8[524288]{0:T(1024)(128)(4,1)S(1)}, s32[]{:S(2)}) async-start(s8[4718592]{0:T(1024)(128)(4,1)} %bitcast.39), calls=%async_computation.3 | async-start | bytes 1048576
  71.0 4.6 %copy-start = (f32[512,1024]{1,0:T(8,128)}, f32[512,1024]{1,0:T(8,128)S(1)}, u32[]{:S(2)}) copy-start(f32[512,1024]{1,0:T(8,128)S(1)} %get-tuple-element.49.h_in) | copy-start | bytes 6291460
  71.0 4.6 %slice-start.4 = ((s8[4718592]{0:T(1024)(128)(4,1)}), s8[4194304]{0:T(1024)(128)(4,1)S(1)}, s32[]{:S(2)}) async-start(s8[4718592]{0:T(1024)(128)(4,1)} %bitcast.41), calls=%async_computation.4 | async-start | bytes 8388608
  71.3 4.3 %copy-start.9 = (bf16[512,1024]{1,0:T(8,128)(2,1)}, bf16[512,1024]{1,0:T(8,128)(2,1)S(1)}, u32[]{:S(2)}) copy-start(bf16[512,1024]{1,0:T(8,128)(2,1)S(1)} %multiply_convert_fusion.3.hn_in) | copy-start | bytes 3145732
  71.3 4.5 %slice-start.5 = ((s8[4718592]{0:T(1024)(128)(4,1)}), s8[524288]{0:T(1024)(128)(4,1)S(1)}, s32[]{:S(2)}) async-start(s8[4718592]{0:T(1024)(128)(4,1)} %bitcast.41), calls=%async_computation.5 | async-start | bytes 1048576
  71.3 8.8 %slice-start = ((s8[4718592]{0:T(1024)(128)(4,1)}), s8[4194304]{0:T(1024)(128)(4,1)S(1)}, s32[]{:S(2)}) async-start(s8[4718592]{0:T(1024)(128)(4,1)} %bitcast.37), calls=%async_computation | async-start | bytes 8388608
  75.8 4.3 %slice-start.1 = ((s8[4718592]{0:T(1024)(128)(4,1)}), s8[524288]{0:T(1024)(128)(4,1)S(1)}, s32[]{:S(2)}) async-start(s8[4718592]{0:T(1024)(128)(4,1)} %bitcast.37), calls=%async_computation.1 | async-start | bytes 1048576
  88.4 2.6 %copy-start.24 = (bf16[512,2304]{1,0:T(8,128)(2,1)}, bf16[512,2304]{1,0:T(8,128)(2,1)S(1)}, u32[]{:S(2)}) copy-start(bf16[512,2304]{1,0:T(8,128)(2,1)S(1)} %get-tuple-element.54.u_in) | copy-start | bytes 7077892
  92.0 103.6 %collective-permute-start.3 = (bf16[512,512]{1,0:T(8,128)(2,1)S(1)}, bf16[512,512]{1,0:T(8,128)(2,1)}, u32[]{:S(2)}, u32[]{:S(2)}) collective-permute-start(bf16[512,512]{1,0:T(8,128)(2,1)S(1)} %constant_dynamic-slice_fusion), channel_id=1, source_target_pairs={{0,1},{1,0},{2,3},{3,2},{4,5},{5,4},{6,7},{7,6},{8,9},{9,8},{10,11... | collective-permute-start | bytes 1572872 | tf_op jit(solution)/shard_map/ppermute | solution.py:630
  191.2 7.0 %copy-start.10 = (f32[512,512]{1,0:T(8,128)S(1)}, f32[512,512]{1,0:T(8,128)}, u32[]{:S(2)}) copy-start(f32[512,512]{1,0:T(8,128)} %get-tuple-element.77) | copy-start | bytes 3145732
  195.6 3.6 %copy-start.16 = (f32[16,512]{1,0:T(8,128)S(1)}, f32[16,512]{1,0:T(8,128)}, u32[]{:S(2)}) copy-start(f32[16,512]{1,0:T(8,128)} %get-tuple-element.24) | copy-start | bytes 98308
  195.6 4.2 %copy-start.15 = (f32[16,2304]{1,0:T(8,128)S(1)}, f32[16,2304]{1,0:T(8,128)}, u32[]{:S(2)}) copy-start(f32[16,2304]{1,0:T(8,128)} %get-tuple-element.83) | copy-start | bytes 442372
  195.6 4.9 %copy-start.14 = (f32[16,2304]{1,0:T(8,128)S(1)}, f32[16,2304]{1,0:T(8,128)}, u32[]{:S(2)}) copy-start(f32[16,2304]{1,0:T(8,128)} %get-tuple-element.84) | copy-start | bytes 442372
  195.6 5.5 %copy-start.13 = (f32[16,2304]{1,0:T(8,128)S(1)}, f32[16,2304]{1,0:T(8,128)}, u32[]{:S(2)}) copy-start(f32[16,2304]{1,0:T(8,128)} %get-tuple-element.27) | copy-start | bytes 442372
  (4 other events, 4.9 us)

commit v2 on v1

v2 whole, which is shorter than its diff:
```python
import jax
import jax.numpy as jnp
from jax import lax
from jax.experimental import pallas as pl
from jax.experimental.pallas import tpu as pltpu
from jax.sharding import PartitionSpec as P

SEQS = 2
NORM_EPS = 1e-05
MESH = pl.DeviceIdType.MESH
F32 = jnp.float32
BF16 = jnp.bfloat16
VMEM_LIMIT = 66_000_000

ROWS = 512
D = 1024
HALF = 512
FFH = 2304
WF = 1152
WT = 1024
KEYS = ("c", "e1p", "e1m", "e2p", "e2m", "f1p", "f1m", "f2p", "f2m", "h")


def nt(a, b):
    return lax.dot_general(a, b, (((1,), (1,)), ((), ())), preferred_element_type=F32)


def nn(a, b):
    return jnp.dot(a, b, preferred_element_type=F32)


def mod(a, n):
    return lax.rem(a, n)


def neighbours():
    s = lax.axis_index("seq")
    sh = lax.axis_index("shard")
    y, zh, x, c = s // 16, mod(s // 8, 2), mod(s // 2, 4), mod(s, 2)

    def at(y_, zh_, x_, c_):
        return (((y_ * 2 + zh_) * 4 + x_) * 2 + c_, sh)

    to = {
        "z": (s, 1 - sh),
        "c": at(y, zh, x, 1 - c),
        "xp": at(y, zh, mod(x + 1, 4), c),
        "xm": at(y, zh, mod(x + 3, 4), c),
        "x2": at(y, zh, mod(x + 2, 4), c),
        "yp": at(mod(y + 1, 4), zh, x, c),
        "ym": at(mod(y + 3, 4), zh, x, c),
        "y2": at(mod(y + 2, 4), zh, x, c),
        "zh": at(y, 1 - zh, x, c),
        "nx": (mod(s + 1, 64), sh),
        "pv": (mod(s + 63, 64), sh),
    }
    return s, sh, (y, zh, x, c), to


def greet(to, names):
    barrier = pltpu.get_barrier_semaphore()
    for name in names:
        pl.semaphore_signal(barrier, inc=1, device_id=to[name], device_id_type=MESH)
    pl.semaphore_wait(barrier, len(names))


def send(src, dst, sems, rems, device):
    return pltpu.make_async_remote_copy(
        src_ref=src,
        dst_ref=dst,
        send_sem=sems,
        recv_sem=rems,
        device_id=device,
        device_id_type=MESH,
    )


def added(dst, *others):
    blocks = dst.shape[0]

    def step(i, _):
        total = dst[i].astype(F32)
        for o in others:
            total = total + o[i].astype(F32)
        dst[i] = total.astype(BF16)
        return 0

    lax.fori_loop(0, blocks, step, 0)


class Half:
    def __init__(self, first, to, s_ref, bufs, sems, rems):
        self.first, self.to, self.s, self.b = first, to, s_ref, bufs
        self.sems, self.rems = sems, rems
        self.ups = ("xp", "xm", "yp", "ym") if first == 0 else ("yp", "ym", "xp", "xm")
        self.sent = []
        self.made = {}

    def view(self, i, j):
        i, j = (i, j) if self.first == 0 else (j, i)
        i = slice(None) if i is None else (pl.ds(*i) if isinstance(i, tuple) else i)
        j = slice(None) if j is None else (pl.ds(*j) if isinstance(j, tuple) else j)
        return self.s.at[i, j]

    def go(self, key, src, dst, name):
        k = KEYS.index(key)
        copy = send(src, dst, self.sems.at[k], self.rems.at[k], self.to[name])
        copy.start()
        self.made[key] = copy

    def arrived(self, *keys):
        for k in keys:
            self.made[k].wait_recv()

    def core(self, g_ref):
        self.go("c", g_ref, self.s, "c")

    def e1(self):
        self.go("e1p", self.view(2, (0, 2)), self.b["e1p"], self.ups[0])
        self.go("e1m", self.view(2, (2, 2)), self.b["e1m"], self.ups[1])

    def e2(self):
        self.arrived("e1p", "e1m")
        added(self.view(1, (0, 2)), self.b["e1p"])
        self.go("e2p", self.view(1, None), self.b["e2p"], self.ups[0])
        added(self.view(3, (2, 2)), self.b["e1m"])
        self.go("e2m", self.view(3, None), self.b["e2m"], self.ups[1])

    def f1(self):
        self.arrived("e2p", "e2m")
        added(self.view(0, None), self.b["e2p"], self.b["e2m"])
        t = self.view(0, 2)
        self.go("f1p", t.at[pl.ds(0, 16)], self.b["f1p"], self.ups[2])
        self.go("f1m", t.at[pl.ds(16, 16)], self.b["f1m"], self.ups[3])

    def f2(self):
        self.arrived("f1p", "f1m")
        t1, t3 = self.view(0, 1), self.view(0, 3)
        t1[0:16, :] = (t1[0:16, :].astype(F32) + self.b["f1p"][...].astype(F32)).astype(BF16)
        self.go("f2p", t1, self.b["f2p"], self.ups[2])
        t3[16:32, :] = (t3[16:32, :].astype(F32) + self.b["f1m"][...].astype(F32)).astype(BF16)
        self.go("f2m", t3, self.b["f2m"], self.ups[3])

    def hop(self):
        self.arrived("f2p", "f2m")
        t = self.view(0, 0)
        t[...] = (
            t[...].astype(F32) + self.b["f2p"][...].astype(F32) + self.b["f2m"][...].astype(F32)
        ).astype(BF16)
        self.go("h", t.at[pl.ds(16, 16)], self.b["h"], "zh")

    def result(self):
        self.arrived("h")
        return self.view(0, 0)[0:16, :].astype(F32) + self.b["h"][...].astype(F32)

    def finish(self):
        for k in KEYS:
            if k != "c":
                self.made[k].wait_send()


def half_bufs(n, w):
    return [
        pltpu.VMEM((n, 4, 4, 32, w), BF16),
        pltpu.VMEM((n, 2, 2, 32, w), BF16),
        pltpu.VMEM((n, 2, 4, 32, w), BF16),
        pltpu.VMEM((n, 2, 16, w), BF16),
        pltpu.VMEM((n, 2, 32, w), BF16),
        pltpu.VMEM((n, 16, w), BF16),
    ]


def halves(n, to, refs, sems, rems, base):
    s, e1, e2, f1, f2, h = refs
    out = []
    for i in range(n):
        bufs = {
            "e1p": e1.at[i, 0],
            "e1m": e1.at[i, 1],
            "e2p": e2.at[i, 0],
            "e2m": e2.at[i, 1],
            "f1p": f1.at[i, 0],
            "f1m": f1.at[i, 1],
            "f2p": f2.at[i, 0],
            "f2m": f2.at[i, 1],
            "h": h.at[i],
        }
        out.append(Half(i % 2, to, s.at[i], bufs, sems.at[base + i], rems.at[base + i]))
    return out


def tiles(n, body):
    lax.fori_loop(0, n, lambda i, _: (body(i), 0)[1], 0)


def mult(i, n):
    return pl.multiple_of(i * n, n)


def flat(v):
    return v.reshape(-1, v.shape[-1])


def turned(perm, at, a_ref):
    for (block, col), dst in zip(perm, at):
        rows = flat(block[:, :, :, pl.ds(col, D)])
        dst[...] = nt(rows, a_ref[...]).astype(BF16)


def order_matrix(perm, place):
    y, zh, x, c = place
    k = lax.broadcasted_iota(jnp.int32, (1, D), 1)
    k16 = k >> 4
    crel = ((k16 & 1) - c) & 1
    xrel = (((k16 >> 1) & 3) - x) & 3
    zrel = (((k16 >> 3) & 1) - zh) & 1
    yrel = ((k16 >> 4) - y) & 3
    pos = (((crel * 4 + xrel) * 4 + yrel) * 2 + zrel) * 16 + (k & 15)

    for b, (block, col) in enumerate(perm):
        for q in range(4):

            def step(t, b=b, q=q, block=block, col=col):
                r = lax.broadcasted_iota(jnp.int32, (32, D), 0) + (b * 512 + q * 128 + t * 32)
                block[q, t, :, pl.ds(col, D)] = jnp.where(r == pos, 1.0, 0.0).astype(BF16)

            tiles(4, step)


def block_kernel(
    tok_in, cot_in, win_in, wout_in, wg_in, wu_in, wd_in, cw, g1, g2,
    bo, tg, gate_o, up_o, down_o, out_o, in_o, vec_o,
    wbuf, wd, win, wout, xv, cot, hv, p, bx, yv, u, da, db, dm, dsend, drecv, mrecv,
    dce, dp, own, xs, xr, br, rd, rds, rdr, r1v, acc, vs, vx, vy, halo_p, halo_n,
    s_f, e1_f, e2_f, f1_f, f2_f, h_f, s_t, e1_t, e2_t, f1_t, f2_t, h_t,
    lsem, rs_s, rs_r, ms, mr,
):
    s, sh, place, to = neighbours()
    mine = pl.ds(mult(sh, 512), 512)
    theirs = pl.ds(mult(1 - sh, 512), 512)
    loads = []

    def load(src, dst):
        copy = pltpu.make_async_copy(src, dst, lsem.at[len(loads)])
        copy.start()
        loads.append(copy)
        return copy

    made = []

    def go(src, dst, name):
        k = len(made)
        copy = send(src, dst, ms.at[k], mr.at[k], to[name])
        copy.start()
        made.append(copy)
        return copy

    l_tok = load(tok_in, xv.at[:, mine])
    l_win = load(win_in, win)
    l_cot = load(cot_in, cot.at[:, mine])
    l_wout = load(wout_in, wout)
    l_wg = load(wg_in, wbuf.at[0])
    l_wu = load(wu_in, wbuf.at[1])
    l_wd = load(wd_in, wd)
    greet(to, ("z", "c", "xp", "xm", "x2", "yp", "ym", "y2", "zh", "nx", "pv"))
    parts = [pl.ds(0, 256), pl.ds(256, 256)]
    z_tok = [None, None]
    for r in (1, 0):
        z_tok[r] = go(tok_in.at[parts[r]], xv.at[parts[r], mine], "z")

    l_tok.wait()
    l_win.wait()

    def project(r):
        z_tok[r].wait_recv()

        def step(t):
            rows = pl.ds(pl.multiple_of(r * 256 + t * 32, 32), 32)
            xf = xv[rows, :].astype(F32)
            r1 = lax.rsqrt(jnp.mean(xf * xf, axis=-1, keepdims=True) + NORM_EPS)
            r1v[rows, :] = jnp.broadcast_to(r1, (32, 128))
            dm[rows, :] = (xf * r1 * g1[...]).astype(BF16)

        tiles(8, step)
        rows = parts[r]
        for n in range(2):
            c = 256 * n
            tb = nn(dm[rows, :], win[:, c : c + 256])
            tx = nn(dm[rows, :], win[:, 1024 + c : 1280 + c])
            p[rows, c : c + 256] = tb.astype(BF16)
            p[rows, 1024 + c : 1280 + c] = tx.astype(BF16)
            bx[pl.ds(8 + 256 * r, 256), c : c + 256] = tb * tx
            tc = nn(dm[rows, :], win[:, 512 + c : 768 + c])
            own[rows, c : c + 256] = tc
            p[rows, 512 + c : 768 + c] = tc.astype(BF16)

    project(1)
    z_halo = go(bx.at[pl.ds(512, 8)], halo_p, "nx")
    project(0)
    z_cot = go(cot_in, cot.at[:, mine], "z")
    z_halo.wait_recv()
    bx[0:8, :] = jnp.where(mod(s, 32) == 0, 0.0, halo_p[...])
    l_wout.wait()
    z_m = []
    for r in range(2):

        def step(t, r=r):
            base = r * 256 + t * 64
            w = bx[pl.ds(pl.multiple_of(base, 64), 72), :]
            conv = cw[0:1, :] * w[6:70] + cw[1:2, :] * w[7:71] + cw[2:3, :] * w[8:72]
            rows = pl.ds(pl.multiple_of(base, 64), 64)
            yv[rows, :] = (own[rows, :] * conv).astype(BF16)

        tiles(4, step)
        rows = parts[r]
        for n in range(2):
            cols = pl.ds(512 * n, 512)
            dsend[rows, cols] = nn(yv[rows, :], wout[:, cols]).astype(BF16)
        z_m.append(go(dsend.at[rows], mrecv.at[rows], "z"))

    l_cot.wait()
    z_cot.wait_recv()
    for l in (l_wg, l_wu, l_wd):
        l.wait()
    z_dhn = []
    for r in range(2):
        z_m[r].wait_recv()

        def step(t, r=r):
            rows = pl.ds(pl.multiple_of(r * 256 + t * 32, 32), 32)
            hf = xv[rows, :].astype(F32) + dsend[rows, :].astype(F32) + mrecv[rows, :].astype(F32)
            hv[rows, :] = hf
            r2 = lax.rsqrt(jnp.mean(hf * hf, axis=-1, keepdims=True) + NORM_EPS)
            dm[rows, :] = (hf * r2 * g2[...]).astype(BF16)

        tiles(8, step)
        rows = parts[r]
        for n in range(9):
            cols = pl.ds(256 * n, 256)
            a = nn(dm[rows, :], flat(wbuf[0, :, :, :, :, cols]))
            b = nn(dm[rows, :], flat(wbuf[1, :, :, :, :, cols]))
            du = nt(cot[rows, :], wd[cols, :])
            sig = jax.nn.sigmoid(a)
            silu = a * sig
            u[rows, cols] = (silu * b).astype(BF16)
            db[rows, cols] = (du * silu).astype(BF16)
            da[rows, cols] = (du * b * (sig + silu * (1.0 - sig))).astype(BF16)
        z_m[r].wait_send()
        for n in range(2):
            t = nt(da[rows, :], flat(wbuf[0, n])) + nt(db[rows, :], flat(wbuf[1, n]))
            dsend[rows, pl.ds(512 * n, 512)] = t.astype(BF16)
        z_dhn.append(go(dsend.at[rows], drecv.at[rows], "z"))

    xs[...] = nn(u[...], wd[:, theirs]).astype(BF16)
    z_out = go(xs, br, "z")
    own[...] = nn(u[...], wd[:, mine]) + hv[:, mine]

    perm = [(wbuf.at[1, 1], 0), (wbuf.at[1, 1], 1024)]
    order_matrix(perm, place)

    def pair(k):
        rows = pl.ds(512 * k, 512)
        return wd.at[rows, pl.ds(0, 512)], wd.at[rows, pl.ds(512, 512)]

    hnt, cott, xnt, dmt = pair(0), pair(1), pair(2), pair(3)
    turned(perm, hnt, dm)
    ffn = halves(6, to, (s_f, e1_f, e2_f, f1_f, f2_f, h_f), rs_s, rs_r, 0)
    tail = halves(2, to, (s_t, e1_t, e2_t, f1_t, f2_t, h_t), rs_s, rs_r, 6)
    ffn_parts = [(hnt, da), (hnt, db), (cott, u)]
    slots = [wbuf.at[0, 0], wbuf.at[0, 1], wbuf.at[1, 0]]

    def ffn_send(k):
        at, b = ffn_parts[k]
        for n in range(3):
            cols = pl.ds(768 * n, 768)
            t = nn(at[1][...], b[:, cols])
            slots[k][:, :, :, cols] = t.astype(BF16).reshape(4, 4, 32, 768)
            if n == 1:
                ffn[2 * k].core(slots[k].at[:, :, :, pl.ds(0, WF)])
        ffn[2 * k + 1].core(slots[k].at[:, :, :, pl.ds(WF, WF)])

    def into(ref, cols, t):
        ref[:, :, :, cols] = (
            t.reshape(4, 4, 32, t.shape[-1]) + ref[:, :, :, cols].astype(F32)
        ).astype(BF16)

    def ffn_keep(k):
        at, b = ffn_parts[k]
        lo, hi = s_f.at[2 * k], s_f.at[2 * k + 1]
        ffn[2 * k].arrived("c")
        t = nn(at[0][...], b[:, 0:768])
        into(lo, pl.ds(0, 768), t)
        ffn[2 * k + 1].arrived("c")
        t = nn(at[0][...], b[:, 768:1536])
        into(lo, pl.ds(768, 384), t[:, 0:384])
        ffn[2 * k].e1()
        into(hi, pl.ds(0, 384), t[:, 384:768])
        t = nn(at[0][...], b[:, 1536:2304])
        into(hi, pl.ds(384, 768), t)
        ffn[2 * k + 1].e1()

    ffn_send(0)
    ffn_send(1)
    ffn_keep(0)
    turned(perm, cott, cot)
    ffn_send(2)
    ffn_keep(1)
    for i in range(2):
        ffn[i].e2()

    acc[...] = jnp.zeros_like(acc)

    def xstep(t):
        rows = pl.ds(mult(t, 32), 32)
        dm[rows, :] = (xv[rows, :].astype(F32) * r1v[rows, 0:1] * g1[...]).astype(BF16)

    tiles(ROWS // 32, xstep)
    turned(perm, xnt, dm)
    z_out.wait_recv()
    bo[...] = (own[...] + br[...].astype(F32)).astype(BF16)

    def mixer(r):
        z_dhn[r].wait_recv()

        def step(t):
            rows = pl.ds(pl.multiple_of(r * 256 + t * 32, 32), 32)
            hf = hv[rows, :]
            r2 = lax.rsqrt(jnp.mean(hf * hf, axis=-1, keepdims=True) + NORM_EPS)
            dhn = dsend[rows, :].astype(F32) + drecv[rows, :].astype(F32)
            acc[0:8, :] += (dhn * hf * r2).reshape(4, 8, D).sum(axis=0)
            scaled = dhn * g2[...]
            dot = jnp.mean(scaled * hf, axis=-1, keepdims=True)
            d = cot[rows, :].astype(F32) + r2 * scaled - hf * (r2 * r2 * r2 * dot)
            dm[rows, :] = d.astype(BF16)
            tg[rows, :] = jnp.where(sh == 0, d[:, 0:512], d[:, 512:1024])

        tiles(8, step)
        rows = parts[r]
        dy = nt(dm[rows, :], wout[...])
        own[rows, :] = dy
        dce[rows, :] = dy * p[rows, 512:1024].astype(F32)

    mixer(0)
    back = go(dce.at[pl.ds(0, 8)], halo_n, "pv")
    ffn_keep(2)
    for i in range(2, 4):
        ffn[i].e2()
    mixer(1)
    back.wait_recv()
    dce[512:520, :] = jnp.where(mod(s, 32) == 31, 0.0, halo_n[...])

    def dstep(t):
        rows = pl.ds(mult(t, 64), 64)
        ext = pl.ds(mult(t, 64), 72)
        dc = dce[ext, :]
        w = bx[ext, :]
        d0 = dc[0:64]
        b2, b1, b0 = w[6:70], w[7:71], w[8:72]
        acc[8:16, 0:512] += (d0 * b2).reshape(8, 8, 512).sum(axis=0)
        acc[16:24, 0:512] += (d0 * b1).reshape(8, 8, 512).sum(axis=0)
        acc[24:32, 0:512] += (d0 * b0).reshape(8, 8, 512).sum(axis=0)
        conv = cw[0:1, :] * b2 + cw[1:2, :] * b1 + cw[2:3, :] * b0
        dbx = cw[2:3, :] * d0 + cw[1:2, :] * dc[1:65] + cw[0:1, :] * dc[2:66]
        dp[rows, 0:512] = (dbx * p[rows, 1024:1536].astype(F32)).astype(BF16)
        dp[rows, 512:1024] = (own[rows, :] * conv).astype(BF16)
        dp[rows, 1024:1536] = (dbx * p[rows, 0:512].astype(F32)).astype(BF16)

    tiles(8, dstep)

    rd[...] = jnp.zeros_like(rd)
    z_out.wait_send()

    def dxn(half, dst):
        for n in range(2):
            wr = pl.ds(pl.multiple_of(half * 512 + n * 256, 256), 256)
            for rows in parts:
                t = nt(dp[rows, :], win[wr, :])
                tx = t * xv[rows, wr].astype(F32)
                rd[rows, :] += jnp.broadcast_to(
                    jnp.sum(tx * g1[:, wr], axis=-1, keepdims=True), (256, 128)
                )
                acc[32:40, wr] += (tx * r1v[rows, 0:1]).reshape(32, 8, 256).sum(axis=0)
                dst[rows, pl.ds(256 * n, 256)] = t.astype(dst.dtype)

    dxn(1 - sh, xs)
    z_dxn = go(xs, xr, "z")
    dxn(sh, own)
    hi = rd[...].astype(BF16)
    lo = (rd[...] - hi.astype(F32)).astype(BF16)
    lane = lax.broadcasted_iota(jnp.int32, (ROWS, 128), 1)
    rds[...] = jnp.where(lane < 64, hi.astype(F32), lo.astype(F32)).astype(BF16)
    z_rd = go(rds, rdr, "z")

    row = lax.broadcasted_iota(jnp.int32, (8, D), 0)

    def total(lo_):
        t = jnp.sum(acc[lo_ : lo_ + 8, :], axis=0, keepdims=True)
        return jnp.broadcast_to(t, (8, D))

    v = jnp.where(row == 0, total(32), 0.0)
    v = jnp.where(row == 1, 0.5 * total(0), v)
    v = jnp.where(row == 2, total(8), v)
    v = jnp.where(row == 3, total(16), v)
    v = jnp.where(row == 4, total(24), v)
    vs[0] = v
    v_z = go(vs.at[0], vs.at[5], "z")

    turned(perm, dmt, dm)

    def tail_gemm(i, k, store):
        store(pl.ds(0, 256), nn(dmt[k][...], yv[:, 256 * i : 256 * i + 256]))
        store(pl.ds(256, 768), nn(xnt[k][...], dp[:, 768 * i : 768 * i + 768]))

    for i in range(2):
        ffn[i].made["c"].wait_send()

        def store(cols, t, i=i):
            here = pl.ds(i * WF + cols.start, cols.size)
            slots[0][:, :, :, here] = t.astype(BF16).reshape(4, 4, 32, cols.size)

        tail_gemm(i, 1, store)
        tail[i].core(slots[0].at[:, :, :, pl.ds(i * WF, WT)])

    def tail_keep(i):
        tail[i].arrived("c")
        tail_gemm(i, 0, lambda cols, t: into(s_t.at[i], cols, t))
        tail[i].e1()

    for i in range(4, 6):
        ffn[i].e2()
    for i in range(2):
        ffn[i].f1()
    tail_keep(0)
    tail_keep(1)
    v_z.wait_recv()
    vs[1] = vs[0] + jnp.where(row < 2, vs[5], 0.0)
    v_c = go(vs.at[1], vs.at[6], "c")
    for i in range(2, 4):
        ffn[i].f1()
    for i in range(2):
        tail[i].e2()
    for i in range(2):
        ffn[i].f2()
    v_c.wait_recv()
    vs[2] = vs[1] + vs[6]
    y, zh, x, c = place
    vx[x] = vs[2]
    v_x = [go(vs.at[2], vx.at[x], n) for n in ("xp", "xm", "x2")]
    for i in range(4, 6):
        ffn[i].f1()
    for i in range(2, 4):
        ffn[i].f2()

    z_dxn.wait_recv()
    z_rd.wait_recv()

    def tstep(t):
        rows = pl.ds(mult(t, 64), 64)
        r1 = r1v[rows, 0:1]
        d = own[rows, :] + xr[rows, :].astype(F32)
        q = rdr[rows, :].astype(F32)
        mean = (rd[rows, 0:1] + q[:, 0:1] + q[:, 64:65]) * (1.0 / D)
        xo = xv[rows, mine].astype(F32)
        tg[rows, :] += r1 * (d * g1[:, mine]) - xo * (r1 * r1 * r1 * mean)

    tiles(8, tstep)

    for i in range(4, 6):
        ffn[i].f2()
    for i in range(2):
        tail[i].f1()
    for w in v_x:
        w.wait_recv()
    vs[3] = (vx[0] + vx[1]) + (vx[2] + vx[3])
    vy[y] = vs[3]
    v_y = [go(vs.at[3], vy.at[y], n) for n in ("yp", "ym", "y2")]
    for i in range(6):
        ffn[i].hop()
    for i in range(2):
        tail[i].f2()
    for w in v_y:
        w.wait_recv()
    vs[4] = (vy[0] + vy[1]) + (vy[2] + vy[3])
    v_h = go(vs.at[4], vs.at[7], "zh")
    for i, o in enumerate((gate_o, up_o, down_o)):
        o[:, 0:WF] = ffn[2 * i].result()
        o[:, WF : 2 * WF] = ffn[2 * i + 1].result()
    for i in range(2):
        tail[i].hop()
    for i in range(2):
        t = tail[i].result()
        out_o[:, 256 * i : 256 * i + 256] = t[:, 0:256]
        in_o[:, 768 * i : 768 * i + 768] = t[:, 256:1024]
    v_h.wait_recv()
    vec_o[...] = vs[4] + vs[7]
    for q in made:
        if all(q is not d for d in (*z_m, z_out)):
            q.wait_send()
    for q in ffn + tail:
        q.finish()
    for q in ffn[2:] + tail:
        q.made["c"].wait_send()


def block(*args):
    hbm = pl.BlockSpec(memory_space=pl.ANY)
    vm = pl.BlockSpec(memory_space=pltpu.VMEM)
    sds = jax.ShapeDtypeStruct
    scratch = [
        pltpu.VMEM((2, 2, 4, 4, 32, FFH), BF16),
        pltpu.VMEM((FFH, D), BF16),
        pltpu.VMEM((D, 3 * HALF), BF16),
        pltpu.VMEM((HALF, D), BF16),
        pltpu.VMEM((ROWS, D), BF16),
        pltpu.VMEM((ROWS, D), BF16),
        pltpu.VMEM((ROWS, D), F32),
        pltpu.VMEM((ROWS, 3 * HALF), BF16),
        pltpu.VMEM((ROWS + 8, HALF), F32),
        pltpu.VMEM((ROWS, HALF), BF16),
        pltpu.VMEM((ROWS, FFH), BF16),
        pltpu.VMEM((ROWS, FFH), BF16),
        pltpu.VMEM((ROWS, FFH), BF16),
        pltpu.VMEM((ROWS, D), BF16),
        pltpu.VMEM((ROWS, D), BF16),
        pltpu.VMEM((ROWS, D), BF16),
        pltpu.VMEM((ROWS, D), BF16),
        pltpu.VMEM((ROWS + 8, HALF), F32),
        pltpu.VMEM((ROWS, 3 * HALF), BF16),
        pltpu.VMEM((ROWS, HALF), F32),
        pltpu.VMEM((ROWS, HALF), BF16),
        pltpu.VMEM((ROWS, HALF), BF16),
        pltpu.VMEM((ROWS, HALF), BF16),
        pltpu.VMEM((ROWS, 128), F32),
        pltpu.VMEM((ROWS, 128), BF16),
        pltpu.VMEM((ROWS, 128), BF16),
        pltpu.VMEM((ROWS, 128), F32),
        pltpu.VMEM((40, D), F32),
        pltpu.VMEM((8, 8, D), F32),
        pltpu.VMEM((4, 8, D), F32),
        pltpu.VMEM((4, 8, D), F32),
        pltpu.VMEM((8, HALF), F32),
        pltpu.VMEM((8, HALF), F32),
        *half_bufs(6, WF),
        *half_bufs(2, WT),
        pltpu.SemaphoreType.DMA((8,)),
        pltpu.SemaphoreType.DMA((8, len(KEYS))),
        pltpu.SemaphoreType.DMA((8, len(KEYS))),
        pltpu.SemaphoreType.DMA((24,)),
        pltpu.SemaphoreType.DMA((24,)),
    ]
    return pl.pallas_call(
        block_kernel,
        out_shape=(
            sds((ROWS, HALF), BF16),
            sds((ROWS, HALF), F32),
            sds((16, FFH), F32),
            sds((16, FFH), F32),
            sds((16, FFH), F32),
            sds((16, HALF), F32),
            sds((16, 3 * HALF), F32),
            sds((8, D), F32),
        ),
        in_specs=[hbm] * 7 + [vm] * 3,
        out_specs=(vm,) * 8,
        scratch_shapes=scratch,
        compiler_params=pltpu.CompilerParams(
            collective_id=1, has_side_effects=True, vmem_limit_bytes=VMEM_LIMIT
        ),
        cost_estimate=pl.CostEstimate(
            flops=32_000_000_000, bytes_accessed=24_000_000, transcendentals=0
        ),
        name="block",
    )(*args)


def body(
    tokens, norm_gain, in_weight, conv_weight, out_weight, ffn_gain, gate_weight, up_weight,
    down_weight, cotangent,
):
    bo, tg, gate_g, up_g, down_g, out_g, in_g, vec = block(
        tokens,
        cotangent,
        in_weight.reshape(D, -1),
        out_weight,
        gate_weight.reshape(2, 4, 4, 32, FFH),
        up_weight.reshape(2, 4, 4, 32, FFH),
        down_weight,
        conv_weight.astype(F32),
        norm_gain.astype(F32)[None],
        ffn_gain.astype(F32)[None],
    )
    return (
        bo,
        tg,
        vec[0],
        in_g.reshape(16, 3, HALF),
        vec[2:5, :HALF],
        out_g.T,
        vec[1],
        gate_g,
        up_g,
        down_g.T,
    )


def solution(mesh):
    return jax.shard_map(
        body,
        mesh=mesh,
        in_specs=(
            P("seq", "shard"),
            P(),
            P(None, None, "shard"),
            P(None, "shard"),
            P("shard", None),
            P(),
            P(None, "shard"),
            P(None, "shard"),
            P("shard", None),
            P("seq", "shard"),
        ),
        out_specs=(
            P("seq", "shard"),
            P("seq", "shard"),
            P(),
            P("seq", None, "shard"),
            P(None, "shard"),
            P("shard", "seq"),
            P(),
            P("seq", "shard"),
            P("seq", "shard"),
            P("shard", "seq"),
        ),
        check_vma=False,
    )
```

time: 202 us -> 168 us (0.83)
  Pallas kernels: 97.6 us -> 144 us
  waiting for transfers between devices: 38 us -> 0 us
  matrix products: 23 us -> 0 us
  other arithmetic: 16.1 us -> 1.79 us
  starting transfers between devices: 8.09 us -> 0 us
  local copies, waits for them, and re-layouts: 18 us -> 20.7 us
    pallas_call x1, Pallas kernels: 97.6 us -> 144 us  [block(): pl.pallas_call(block_kernel, out_shape=(sds((ROWS, HALF), BF16), sds((ROW...]
    ppermute x5 -> x0, waiting for transfers between devices: 38 us -> none  [the longest x4 37.2 us: swapped(): return lax.ppermute(block, 'shard', [(0, 1), (1, 0)])]
    dot_general x6 -> x0, matrix products: 23 us -> none  [the longest x1 8.25 us: body(): du = jnp.einsum('td,fd->tf', cot, down_weight, preferred_element_type=F32)]
    ppermute x5 -> x0, starting transfers between devices: 8.09 us -> none  [the longest x4 6.81 us: swapped(): return lax.ppermute(block, 'shard', [(0, 1), (1, 0)])]
    convert_element_type x6 -> x1, other arithmetic: 7.28 us -> 0.6 us  [body(): conv_weight.astype(F32)]
    concatenate x2 -> x0, other arithmetic: 3.57 us -> none  [joined(): jnp.concatenate([jnp.where(first, own, other), jnp.where(first, other, ow...]
    unnamed x68 -> x13, local copies, waits for them, and re-layouts: 10.6 us -> 13.4 us
    select_n x2 -> x0, other arithmetic: 2.66 us -> none  [the longest x1 2.65 us: joined(): jnp.where(first, own, other)]
  transfers between devices with their start and end apart: 5 -> 0, of which waited for: 4 -> 0; matrix products, arithmetic and copies ran while one was open for 7% -> 0% of each run, Pallas kernels for 48% -> 0%
where the time goes in v2:
time: 168 us; the launch traced here: 167 us
  Pallas kernels  144 us (86%)
  local copies, waits for them, and re-layouts  20.7 us (12%)
  other arithmetic  1.79 us (1%)
    pallas_call x1, Pallas kernels, block(): pl.pallas_call(block_kernel, out_shape=(sds((ROWS, HALF), BF16), sds((ROW...  144 us
    unnamed x13, local copies, waits for them, and re-layouts  13.4 us

profile of v2, /device:TPU:0, one launch (start us, length us, event | category | flops | bytes accessed | tf_op | source)
XLA Modules:
  0.0 167.0 jit_solution(10374431327048592734)
XLA Ops:
  0.6 3.2 %copy.22 = bf16[1024,3,512]{0,2,1:T(8,128)(2,1)S(1)} copy(bf16[1024,3,512]{2,0,1:T(8,128)(2,1)} %param.12) | data formatting | bytes 6291456 | tf_op args[2]
  3.8 0.0 copy-start
  3.8 0.0 copy-start.1
  3.9 0.0 copy-start.2
  3.9 3.0 %copy.23.win_in = bf16[1024,1536]{1,0:T(8,128)(2,1)} copy(bf16[1024,1536]{0,1:T(8,128)(2,1)S(1)} %bitcast.13) | data formatting | bytes 6291456 | tf_op jit(solution)/shard_map/reshape | solution.py:683
  6.8 0.0 copy-done
  6.8 0.6 convert_element_type.2.cw
  7.4 0.0 copy-done.1
  7.4 0.6 broadcast_in_dim.14
  8.0 0.0 copy-done.2
  8.0 0.6 broadcast_in_dim.15
  8.6 143.8 %block.1 = (bf16[512,512]{1,0:T(8,128)(2,1)}, f32[512,512]{1,0:T(8,128)}, f32[16,2304]{1,0:T(8,128)}, f32[16,2304]{1,0:T(8,128)}, f32[16,2304]{1,0:T(8,128)}, /*...) custom-call(bf16[512,512]{1,0:T(8,128)(2,1)} %tok_in.1, bf16[512,512]{1,0:T(8,128)(2,1)} %cot_in.1, ...), custom_call_target="tpu_custom_call" | custom-call | flops 32000000000 | bytes 24000000 | tf_op jit(solution)/shard_map/block/pallas_call | solution.py:651
  152.4 1.4 fusion
  153.9 1.3 slice.10
  155.2 1.5 copy.27
  156.7 1.9 %copy.34 = bf16[512,512]{1,0:T(8,128)(2,1)} copy(bf16[512,512]{1,0:T(8,128)(2,1)} %get-tuple-element.58) | data formatting | bytes 1048576
  158.6 2.3 %copy.35 = f32[512,512]{1,0:T(8,128)} copy(f32[512,512]{1,0:T(8,128)} %get-tuple-element.59) | data formatting | bytes 2097152
  160.8 1.4 copy.36
  162.2 1.6 copy.37
  163.8 1.6 copy.38
  165.4 1.6 copy.39
Async XLA Ops:
  3.8 3.0 %copy-start = (bf16[3,512]{1,0:T(4,128)(2,1)S(1)}, bf16[3,512]{1,0:T(4,128)(2,1)}, u32[]{:S(2)}) copy-start(bf16[3,512]{1,0:T(4,128)(2,1)} %param.13) | copy-start | bytes 9220
  3.8 3.6 %copy-start.1 = (bf16[1024]{0:T(1024)(128)(2,1)S(1)}, bf16[1024]{0:T(1024)(128)(2,1)}, u32[]{:S(2)}) copy-start(bf16[1024]{0:T(1024)(128)(2,1)} %param.11) | copy-start | bytes 6148
  3.9 4.2 %copy-start.2 = (bf16[1024]{0:T(1024)(128)(2,1)S(1)}, bf16[1024]{0:T(1024)(128)(2,1)}, u32[]{:S(2)}) copy-start(bf16[1024]{0:T(1024)(128)(2,1)} %param.15) | copy-start | bytes 6148

commit v3 on v2

--- a/solution.py
+++ b/solution.py
@@ -10,7 +10,7 @@
 MESH = pl.DeviceIdType.MESH
 F32 = jnp.float32
 BF16 = jnp.bfloat16
-VMEM_LIMIT = 66_000_000
+VMEM_LIMIT = 67_000_000
 
 ROWS = 512
 D = 1024
@@ -202,9 +202,8 @@
 
 
 def turned(perm, at, a_ref):
-    for (block, col), dst in zip(perm, at):
-        rows = flat(block[:, :, :, pl.ds(col, D)])
-        dst[...] = nt(rows, a_ref[...]).astype(BF16)
+    for k in range(2):
+        at[k][...] = nt(perm[k], a_ref[...]).astype(BF16)
 
 
 def order_matrix(perm, place):
@@ -217,23 +216,22 @@
     yrel = ((k16 >> 4) - y) & 3
     pos = (((crel * 4 + xrel) * 4 + yrel) * 2 + zrel) * 16 + (k & 15)
 
-    for b, (block, col) in enumerate(perm):
-        for q in range(4):
-
-            def step(t, b=b, q=q, block=block, col=col):
-                r = lax.broadcasted_iota(jnp.int32, (32, D), 0) + (b * 512 + q * 128 + t * 32)
-                block[q, t, :, pl.ds(col, D)] = jnp.where(r == pos, 1.0, 0.0).astype(BF16)
-
-            tiles(4, step)
+    for b in range(2):
+
+        def step(t, b=b):
+            r = lax.broadcasted_iota(jnp.int32, (64, D), 0) + (b * 512 + t * 64)
+            perm[b, pl.ds(mult(t, 64), 64), :] = jnp.where(r == pos, 1.0, 0.0).astype(BF16)
+
+        tiles(8, step)
 
 
 def block_kernel(
-    tok_in, cot_in, win_in, wout_in, wg_in, wu_in, wd_in, cw, g1, g2,
-    bo, tg, gate_o, up_o, down_o, out_o, in_o, vec_o,
+    tok_in, cot_in, win_in, wout_in, wg_in, wu_in, wd_in, cw_in, g1_in, g2_in,
+    bo, tg, gate_o, up_o, down_o, out_o, in_o, ng_o, fg_o, cg_o,
     wbuf, wd, win, wout, xv, cot, hv, p, bx, yv, u, da, db, dm, dsend, drecv, mrecv,
-    dce, dp, own, xs, xr, br, rd, rds, rdr, r1v, acc, vs, vx, vy, halo_p, halo_n,
+    dce, perm, xnt, own, xs, xr, br, rd, rds, rdr, r1v, acc, vs, vx, vy, halo_p, halo_n,
     s_f, e1_f, e2_f, f1_f, f2_f, h_f, s_t, e1_t, e2_t, f1_t, f2_t, h_t,
-    lsem, rs_s, rs_r, ms, mr,
+    cw, g1, g2, lsem, rs_s, rs_r, ms, mr,
 ):
     s, sh, place, to = neighbours()
     mine = pl.ds(mult(sh, 512), 512)
@@ -256,23 +254,22 @@
         return copy
 
     l_tok = load(tok_in, xv.at[:, mine])
-    l_win = load(win_in, win)
-    l_cot = load(cot_in, cot.at[:, mine])
-    l_wout = load(wout_in, wout)
-    l_wg = load(wg_in, wbuf.at[0])
-    l_wu = load(wu_in, wbuf.at[1])
-    l_wd = load(wd_in, wd)
+    l_win = [load(win_in.at[j], win.at[:, pl.ds(512 * j, 512)]) for j in range(3)]
     greet(to, ("z", "c", "xp", "xm", "x2", "yp", "ym", "y2", "zh", "nx", "pv"))
     parts = [pl.ds(0, 256), pl.ds(256, 256)]
     z_tok = [None, None]
     for r in (1, 0):
         z_tok[r] = go(tok_in.at[parts[r]], xv.at[parts[r], mine], "z")
 
+    cw[0:3, :] = cw_in[...].astype(F32)
+    g1[...] = g1_in[...].astype(F32).reshape(1, D)
+    g2[...] = g2_in[...].astype(F32).reshape(1, D)
+    l_wout = load(wout_in, wout)
     l_tok.wait()
-    l_win.wait()
+    for l in l_win:
+        l.wait()
 
     def project(r):
-        z_tok[r].wait_recv()
 
         def step(t):
             rows = pl.ds(pl.multiple_of(r * 256 + t * 32, 32), 32)
@@ -294,10 +291,16 @@
             own[rows, c : c + 256] = tc
             p[rows, 512 + c : 768 + c] = tc.astype(BF16)
 
+    z_tok[1].wait_recv()
+    l_cot = load(cot_in, cot.at[:, mine])
+    l_wg = load(wg_in, wbuf.at[0])
+    l_wu = load(wu_in, wbuf.at[1])
+    l_wd = load(wd_in, wd)
     project(1)
     z_halo = go(bx.at[pl.ds(512, 8)], halo_p, "nx")
+    z_tok[0].wait_recv()
+    z_cot = go(cot_in, cot.at[:, mine], "z")
     project(0)
-    z_cot = go(cot_in, cot.at[:, mine], "z")
     z_halo.wait_recv()
     bx[0:8, :] = jnp.where(mod(s, 32) == 0, 0.0, halo_p[...])
     l_wout.wait()
@@ -317,6 +320,9 @@
             cols = pl.ds(512 * n, 512)
             dsend[rows, cols] = nn(yv[rows, :], wout[:, cols]).astype(BF16)
         z_m.append(go(dsend.at[rows], mrecv.at[rows], "z"))
+
+    order_matrix(perm, place)
+    turned(perm, [xnt.at[0], xnt.at[1]], dm)
 
     l_cot.wait()
     z_cot.wait_recv()
@@ -329,7 +335,7 @@
         def step(t, r=r):
             rows = pl.ds(pl.multiple_of(r * 256 + t * 32, 32), 32)
             hf = xv[rows, :].astype(F32) + dsend[rows, :].astype(F32) + mrecv[rows, :].astype(F32)
-            hv[rows, :] = hf
+            hv[rows, :] = hf.astype(BF16)
             r2 = lax.rsqrt(jnp.mean(hf * hf, axis=-1, keepdims=True) + NORM_EPS)
             dm[rows, :] = (hf * r2 * g2[...]).astype(BF16)
 
@@ -351,18 +357,10 @@
             dsend[rows, pl.ds(512 * n, 512)] = t.astype(BF16)
         z_dhn.append(go(dsend.at[rows], drecv.at[rows], "z"))
 
-    xs[...] = nn(u[...], wd[:, theirs]).astype(BF16)
-    z_out = go(xs, br, "z")
-    own[...] = nn(u[...], wd[:, mine]) + hv[:, mine]
-
-    perm = [(wbuf.at[1, 1], 0), (wbuf.at[1, 1], 1024)]
-    order_matrix(perm, place)
-
-    def pair(k):
-        rows = pl.ds(512 * k, 512)
-        return wd.at[rows, pl.ds(0, 512)], wd.at[rows, pl.ds(512, 512)]
-
-    hnt, cott, xnt, dmt = pair(0), pair(1), pair(2), pair(3)
+    hnt = [mrecv.at[:, pl.ds(512 * k, 512)] for k in range(2)]
+    cott = [wd.at[pl.ds(0, 512), pl.ds(512 * k, 512)] for k in range(2)]
+    dmt = [wd.at[pl.ds(512, 512), pl.ds(512 * k, 512)] for k in range(2)]
+    dp = wbuf.at[1, 1]
     turned(perm, hnt, dm)
     ffn = halves(6, to, (s_f, e1_f, e2_f, f1_f, f2_f, h_f), rs_s, rs_r, 0)
     tail = halves(2, to, (s_t, e1_t, e2_t, f1_t, f2_t, h_t), rs_s, rs_r, 6)
@@ -401,30 +399,17 @@
 
     ffn_send(0)
     ffn_send(1)
+    xs[...] = nn(u[...], wd[:, theirs]).astype(BF16)
+    bo[...] = (nn(u[...], wd[:, mine]) + hv[:, mine].astype(F32)).astype(BF16)
     ffn_keep(0)
-    turned(perm, cott, cot)
-    ffn_send(2)
-    ffn_keep(1)
-    for i in range(2):
-        ffn[i].e2()
 
     acc[...] = jnp.zeros_like(acc)
 
-    def xstep(t):
-        rows = pl.ds(mult(t, 32), 32)
-        dm[rows, :] = (xv[rows, :].astype(F32) * r1v[rows, 0:1] * g1[...]).astype(BF16)
-
-    tiles(ROWS // 32, xstep)
-    turned(perm, xnt, dm)
-    z_out.wait_recv()
-    bo[...] = (own[...] + br[...].astype(F32)).astype(BF16)
-
     def mixer(r):
-        z_dhn[r].wait_recv()
 
         def step(t):
             rows = pl.ds(pl.multiple_of(r * 256 + t * 32, 32), 32)
-            hf = hv[rows, :]
+            hf = hv[rows, :].astype(F32)
             r2 = lax.rsqrt(jnp.mean(hf * hf, axis=-1, keepdims=True) + NORM_EPS)
             dhn = dsend[rows, :].astype(F32) + drecv[rows, :].astype(F32)
             acc[0:8, :] += (dhn * hf * r2).reshape(4, 8, D).sum(axis=0)
@@ -440,11 +425,16 @@
         own[rows, :] = dy
         dce[rows, :] = dy * p[rows, 512:1024].astype(F32)
 
+    z_dhn[0].wait_recv()
     mixer(0)
     back = go(dce.at[pl.ds(0, 8)], halo_n, "pv")
-    ffn_keep(2)
-    for i in range(2, 4):
+    ffn_keep(1)
+    turned(perm, cott, cot)
+    ffn_send(2)
+    for i in range(2):
         ffn[i].e2()
+    z_dhn[1].wait_recv()
+    z_out = go(xs, br, "z")
     mixer(1)
     back.wait_recv()
     dce[512:520, :] = jnp.where(mod(s, 32) == 31, 0.0, halo_n[...])
@@ -461,20 +451,24 @@
         acc[24:32, 0:512] += (d0 * b0).reshape(8, 8, 512).sum(axis=0)
         conv = cw[0:1, :] * b2 + cw[1:2, :] * b1 + cw[2:3, :] * b0
         dbx = cw[2:3, :] * d0 + cw[1:2, :] * dc[1:65] + cw[0:1, :] * dc[2:66]
-        dp[rows, 0:512] = (dbx * p[rows, 1024:1536].astype(F32)).astype(BF16)
-        dp[rows, 512:1024] = (own[rows, :] * conv).astype(BF16)
-        dp[rows, 1024:1536] = (dbx * p[rows, 0:512].astype(F32)).astype(BF16)
+        at = (t // 2, pl.ds(mod(t, 2) * 2, 2))
+
+        def put(col, v):
+            dp[at[0], at[1], :, col : col + 512] = v.astype(BF16).reshape(2, 32, 512)
+
+        put(0, dbx * p[rows, 1024:1536].astype(F32))
+        put(512, own[rows, :] * conv)
+        put(1024, dbx * p[rows, 0:512].astype(F32))
 
     tiles(8, dstep)
 
     rd[...] = jnp.zeros_like(rd)
-    z_out.wait_send()
 
     def dxn(half, dst):
         for n in range(2):
             wr = pl.ds(pl.multiple_of(half * 512 + n * 256, 256), 256)
-            for rows in parts:
-                t = nt(dp[rows, :], win[wr, :])
+            for r, rows in enumerate(parts):
+                t = nt(flat(dp[2 * r : 2 * r + 2, :, :, 0:1536]), win[wr, :])
                 tx = t * xv[rows, wr].astype(F32)
                 rd[rows, :] += jnp.broadcast_to(
                     jnp.sum(tx * g1[:, wr], axis=-1, keepdims=True), (256, 128)
@@ -482,8 +476,10 @@
                 acc[32:40, wr] += (tx * r1v[rows, 0:1]).reshape(32, 8, 256).sum(axis=0)
                 dst[rows, pl.ds(256 * n, 256)] = t.astype(dst.dtype)
 
-    dxn(1 - sh, xs)
-    z_dxn = go(xs, xr, "z")
+    dxn(1 - sh, mrecv.at[:, pl.ds(0, 512)])
+    z_dxn = go(mrecv.at[:, pl.ds(0, 512)], xr, "z")
+    for i in range(2, 4):
+        ffn[i].e2()
     dxn(sh, own)
     hi = rd[...].astype(BF16)
     lo = (rd[...] - hi.astype(F32)).astype(BF16)
@@ -509,7 +505,7 @@
 
     def tail_gemm(i, k, store):
         store(pl.ds(0, 256), nn(dmt[k][...], yv[:, 256 * i : 256 * i + 256]))
-        store(pl.ds(256, 768), nn(xnt[k][...], dp[:, 768 * i : 768 * i + 768]))
+        store(pl.ds(256, 768), nn(xnt[k], flat(dp[:, :, :, 768 * i : 768 * i + 768])))
 
     for i in range(2):
         ffn[i].made["c"].wait_send()
@@ -526,12 +522,13 @@
         tail_gemm(i, 0, lambda cols, t: into(s_t.at[i], cols, t))
         tail[i].e1()
 
-    for i in range(4, 6):
-        ffn[i].e2()
+    ffn_keep(2)
     for i in range(2):
         ffn[i].f1()
     tail_keep(0)
     tail_keep(1)
+    for i in range(4, 6):
+        ffn[i].e2()
     v_z.wait_recv()
     vs[1] = vs[0] + jnp.where(row < 2, vs[5], 0.0)
     v_c = go(vs.at[1], vs.at[6], "c")
@@ -564,6 +561,8 @@
         tg[rows, :] += r1 * (d * g1[:, mine]) - xo * (r1 * r1 * r1 * mean)
 
     tiles(8, tstep)
+    z_out.wait_recv()
+    bo[...] = (bo[...].astype(F32) + br[...].astype(F32)).astype(BF16)
 
     for i in range(4, 6):
         ffn[i].f2()
@@ -590,11 +589,16 @@
     for i in range(2):
         t = tail[i].result()
         out_o[:, 256 * i : 256 * i + 256] = t[:, 0:256]
-        in_o[:, 768 * i : 768 * i + 768] = t[:, 256:1024]
+        for j in range(6):
+            n = 768 * i + 128 * j
+            in_o[n // 512, :, n % 512 : n % 512 + 128] = t[:, 256 + 128 * j : 384 + 128 * j]
     v_h.wait_recv()
-    vec_o[...] = vs[4] + vs[7]
+    v = vs[4] + vs[7]
+    ng_o[...] = v[0:1, :]
+    fg_o[...] = v[1:2, :]
+    cg_o[...] = v[2:5, 0:512]
     for q in made:
-        if all(q is not d for d in (*z_m, z_out)):
+        if all(q is not d for d in z_m):
             q.wait_send()
     for q in ffn + tail:
         q.finish()
@@ -613,7 +617,7 @@
         pltpu.VMEM((HALF, D), BF16),
         pltpu.VMEM((ROWS, D), BF16),
         pltpu.VMEM((ROWS, D), BF16),
-        pltpu.VMEM((ROWS, D), F32),
+        pltpu.VMEM((ROWS, D), BF16),
         pltpu.VMEM((ROWS, 3 * HALF), BF16),
         pltpu.VMEM((ROWS + 8, HALF), F32),
         pltpu.VMEM((ROWS, HALF), BF16),
@@ -625,7 +629,8 @@
         pltpu.VMEM((ROWS, D), BF16),
         pltpu.VMEM((ROWS, D), BF16),
         pltpu.VMEM((ROWS + 8, HALF), F32),
-        pltpu.VMEM((ROWS, 3 * HALF), BF16),
+        pltpu.VMEM((2, HALF, D), BF16),
+        pltpu.VMEM((2, HALF, ROWS), BF16),
         pltpu.VMEM((ROWS, HALF), F32),
         pltpu.VMEM((ROWS, HALF), BF16),
         pltpu.VMEM((ROWS, HALF), BF16),
@@ -642,7 +647,10 @@
         pltpu.VMEM((8, HALF), F32),
         *half_bufs(6, WF),
         *half_bufs(2, WT),
-        pltpu.SemaphoreType.DMA((8,)),
+        pltpu.VMEM((8, HALF), F32),
+        pltpu.VMEM((1, D), F32),
+        pltpu.VMEM((1, D), F32),
+        pltpu.SemaphoreType.DMA((16,)),
         pltpu.SemaphoreType.DMA((8, len(KEYS))),
         pltpu.SemaphoreType.DMA((8, len(KEYS))),
         pltpu.SemaphoreType.DMA((24,)),
@@ -657,11 +665,13 @@
             sds((16, FFH), F32),
             sds((16, FFH), F32),
             sds((16, HALF), F32),
-            sds((16, 3 * HALF), F32),
-            sds((8, D), F32),
+            sds((3, 16, HALF), F32),
+            sds((1, D), F32),
+            sds((1, D), F32),
+            sds((3, HALF), F32),
         ),
         in_specs=[hbm] * 7 + [vm] * 3,
-        out_specs=(vm,) * 8,
+        out_specs=(vm,) * 10,
         scratch_shapes=scratch,
         compiler_params=pltpu.CompilerParams(
             collective_id=1, has_side_effects=True, vmem_limit_bytes=VMEM_LIMIT
@@ -673,30 +683,51 @@
     )(*args)
 
 
+def settle_kernel(*refs):
+    n = len(refs) // 2
+    for i in range(n):
+        refs[n + i][...] = refs[i][...]
+
+
+def settle(arrays):
+    n = len(arrays)
+    vm = pl.BlockSpec(memory_space=pltpu.VMEM)
+    return pl.pallas_call(
+        settle_kernel,
+        out_shape=tuple(jax.ShapeDtypeStruct(a.shape, a.dtype) for a in arrays),
+        in_specs=[vm] * n,
+        out_specs=(vm,) * n,
+        compiler_params=pltpu.CompilerParams(vmem_limit_bytes=VMEM_LIMIT),
+        name="settle",
+    )(*arrays)
+
+
 def body(
     tokens, norm_gain, in_weight, conv_weight, out_weight, ffn_gain, gate_weight, up_weight,
     down_weight, cotangent,
 ):
-    bo, tg, gate_g, up_g, down_g, out_g, in_g, vec = block(
-        tokens,
-        cotangent,
-        in_weight.reshape(D, -1),
-        out_weight,
-        gate_weight.reshape(2, 4, 4, 32, FFH),
-        up_weight.reshape(2, 4, 4, 32, FFH),
-        down_weight,
-        conv_weight.astype(F32),
-        norm_gain.astype(F32)[None],
-        ffn_gain.astype(F32)[None],
+    bo, tg, gate_g, up_g, down_g, out_g, in_g, ng, fg, cg = settle(
+        block(
+            tokens,
+            cotangent,
+            in_weight.transpose(1, 0, 2),
+            out_weight,
+            gate_weight.reshape(2, 4, 4, 32, FFH),
+            up_weight.reshape(2, 4, 4, 32, FFH),
+            down_weight,
+            conv_weight,
+            norm_gain,
+            ffn_gain,
+        )
     )
     return (
         bo,
         tg,
-        vec[0],
-        in_g.reshape(16, 3, HALF),
-        vec[2:5, :HALF],
+        ng.reshape(D),
+        in_g.transpose(1, 0, 2),
+        cg,
         out_g.T,
-        vec[1],
+        fg.reshape(D),
         gate_g,
         up_g,
         down_g.T,

time: 168 us -> 140 us (0.83)
  local copies, waits for them, and re-layouts: 20.7 us -> 0 us
  Pallas kernels: 144 us -> 139 us
  other arithmetic: 1.79 us -> 0 us
    unnamed x13 -> x0, local copies, waits for them, and re-layouts: 13.4 us -> none
    pallas_call x1, Pallas kernels: 144 us -> 136 us  [block(): pl.pallas_call(block_kernel, out_shape=(sds((ROWS, HALF), BF16), sds((ROW...]
    reshape x2 -> x0, local copies, waits for them, and re-layouts: 4.49 us -> none  [the longest x1 2.95 us: body(): in_weight.reshape(D, -1)]
    pallas_call x0 -> x1, Pallas kernels: none -> 2.93 us  [settle(): pl.pallas_call(settle_kernel, out_shape=tuple((jax.ShapeDtypeStruct(a.sha...]
    slice x2 -> x0, local copies, waits for them, and re-layouts: 2.76 us -> none  [the longest x1 1.44 us: body(): vec[1]]
where the time goes in v3:
time: 140 us
  Pallas kernels  139 us (99%)
    pallas_call x1, Pallas kernels, block(): pl.pallas_call(block_kernel, out_shape=(sds((ROWS, HALF), BF16), sds((ROW...  136 us
    pallas_call x1, Pallas kernels, settle(): pl.pallas_call(settle_kernel, out_shape=tuple((jax.ShapeDtypeStruct(a.sha...  2.93 us

profile of v3, /device:TPU:0, one launch (start us, length us, event | category | flops | bytes accessed | tf_op | source)
XLA Modules:
  0.0 140.0 jit_solution(11643417403790021229)
XLA Ops:
  0.6 136.3 %block.1 = (bf16[512,512]{1,0:T(8,128)(2,1)}, f32[512,512]{1,0:T(8,128)}, f32[16,2304]{1,0:T(8,128)}, f32[16,2304]{1,0:T(8,128)}, f32[16,2304]{1,0:T(8,128)}, /*...) custom-call(bf16[512,512]{1,0:T(8,128)(2,1)} %tok_in.1, ...), custom_call_target="tpu_custom_call" | custom-call | flops 32000000000 | bytes 24000000 | tf_op jit(solution)/shard_map/block/pallas_call | solution.py:659
  136.9 2.9 %settle.1 = (bf16[512,512]{1,0:T(8,128)(2,1)}, f32[512,512]{1,0:T(8,128)}, f32[16,2304]{1,0:T(8,128)}, f32[16,2304]{1,0:T(8,128)}, f32[16,2304]{1,0:T(8,128)}, /...) custom-call(bf16[512,512]{1,0:T(8,128)(2,1)} %get-tuple-element.30.re, ...), custom_call_target="tpu_custom_call" | custom-call | tf_op jit(solution)/shard_map/settle/pallas_call | solution.py:695

commit v4 on v3

--- a/solution.py
+++ b/solution.py
@@ -229,7 +229,7 @@
     tok_in, cot_in, win_in, wout_in, wg_in, wu_in, wd_in, cw_in, g1_in, g2_in,
     bo, tg, gate_o, up_o, down_o, out_o, in_o, ng_o, fg_o, cg_o,
     wbuf, wd, win, wout, xv, cot, hv, p, bx, yv, u, da, db, dm, dsend, drecv, mrecv,
-    dce, perm, xnt, own, xs, xr, br, rd, rds, rdr, r1v, acc, vs, vx, vy, halo_p, halo_n,
+    dce, perm, xnt, cott, own, xr, br, rd, rdr, r1v, acc, vs, vx, vy, halo_p, halo_n,
     s_f, e1_f, e2_f, f1_f, f2_f, h_f, s_t, e1_t, e2_t, f1_t, f2_t, h_t,
     cw, g1, g2, lsem, rs_s, rs_r, ms, mr,
 ):
@@ -288,7 +288,7 @@
             p[rows, 1024 + c : 1280 + c] = tx.astype(BF16)
             bx[pl.ds(8 + 256 * r, 256), c : c + 256] = tb * tx
             tc = nn(dm[rows, :], win[:, 512 + c : 768 + c])
-            own[rows, c : c + 256] = tc
+            dce[rows, c : c + 256] = tc
             p[rows, 512 + c : 768 + c] = tc.astype(BF16)
 
     z_tok[1].wait_recv()
@@ -312,7 +312,7 @@
             w = bx[pl.ds(pl.multiple_of(base, 64), 72), :]
             conv = cw[0:1, :] * w[6:70] + cw[1:2, :] * w[7:71] + cw[2:3, :] * w[8:72]
             rows = pl.ds(pl.multiple_of(base, 64), 64)
-            yv[rows, :] = (own[rows, :] * conv).astype(BF16)
+            yv[rows, :] = (dce[rows, :] * conv).astype(BF16)
 
         tiles(4, step)
         rows = parts[r]
@@ -323,9 +323,11 @@
 
     order_matrix(perm, place)
     turned(perm, [xnt.at[0], xnt.at[1]], dm)
-
     l_cot.wait()
     z_cot.wait_recv()
+    cott = [cott.at[0], cott.at[1]]
+    turned(perm, cott, cot)
+
     for l in (l_wg, l_wu, l_wd):
         l.wait()
     z_dhn = []
@@ -358,9 +360,10 @@
         z_dhn.append(go(dsend.at[rows], drecv.at[rows], "z"))
 
     hnt = [mrecv.at[:, pl.ds(512 * k, 512)] for k in range(2)]
-    cott = [wd.at[pl.ds(0, 512), pl.ds(512 * k, 512)] for k in range(2)]
-    dmt = [wd.at[pl.ds(512, 512), pl.ds(512 * k, 512)] for k in range(2)]
+    dmt = cott
     dp = wbuf.at[1, 1]
+    xs = wbuf.at[1, 1, :, :, :, pl.ds(1536, HALF)]
+    rds = wbuf.at[1, 1, :, :, :, pl.ds(2048, 128)]
     turned(perm, hnt, dm)
     ffn = halves(6, to, (s_f, e1_f, e2_f, f1_f, f2_f, h_f), rs_s, rs_r, 0)
     tail = halves(2, to, (s_t, e1_t, e2_t, f1_t, f2_t, h_t), rs_s, rs_r, 6)
@@ -399,9 +402,12 @@
 
     ffn_send(0)
     ffn_send(1)
-    xs[...] = nn(u[...], wd[:, theirs]).astype(BF16)
-    bo[...] = (nn(u[...], wd[:, mine]) + hv[:, mine].astype(F32)).astype(BF16)
+    ffn_send(2)
     ffn_keep(0)
+    ffn_keep(1)
+    ffn_keep(2)
+    for i in range(2):
+        ffn[i].e2()
 
     acc[...] = jnp.zeros_like(acc)
 
@@ -422,21 +428,20 @@
         tiles(8, step)
         rows = parts[r]
         dy = nt(dm[rows, :], wout[...])
-        own[rows, :] = dy
+        own[rows, :] = dy.astype(BF16)
         dce[rows, :] = dy * p[rows, 512:1024].astype(F32)
 
+    xs[...] = nn(u[...], wd[:, theirs]).astype(BF16).reshape(4, 4, 32, HALF)
     z_dhn[0].wait_recv()
     mixer(0)
     back = go(dce.at[pl.ds(0, 8)], halo_n, "pv")
-    ffn_keep(1)
-    turned(perm, cott, cot)
-    ffn_send(2)
-    for i in range(2):
+    for i in range(2, 4):
         ffn[i].e2()
     z_dhn[1].wait_recv()
     z_out = go(xs, br, "z")
     mixer(1)
     back.wait_recv()
+    back.wait_send()
     dce[512:520, :] = jnp.where(mod(s, 32) == 31, 0.0, halo_n[...])
 
     def dstep(t):
@@ -457,7 +462,7 @@
             dp[at[0], at[1], :, col : col + 512] = v.astype(BF16).reshape(2, 32, 512)
 
         put(0, dbx * p[rows, 1024:1536].astype(F32))
-        put(512, own[rows, :] * conv)
+        put(512, own[rows, :].astype(F32) * conv)
         put(1024, dbx * p[rows, 0:512].astype(F32))
 
     tiles(8, dstep)
@@ -477,14 +482,14 @@
                 dst[rows, pl.ds(256 * n, 256)] = t.astype(dst.dtype)
 
     dxn(1 - sh, mrecv.at[:, pl.ds(0, 512)])
-    z_dxn = go(mrecv.at[:, pl.ds(0, 512)], xr, "z")
-    for i in range(2, 4):
+    for i in range(4, 6):
         ffn[i].e2()
-    dxn(sh, own)
+    dxn(sh, dce)
     hi = rd[...].astype(BF16)
     lo = (rd[...] - hi.astype(F32)).astype(BF16)
     lane = lax.broadcasted_iota(jnp.int32, (ROWS, 128), 1)
-    rds[...] = jnp.where(lane < 64, hi.astype(F32), lo.astype(F32)).astype(BF16)
+    both = jnp.where(lane < 64, hi.astype(F32), lo.astype(F32))
+    rds[...] = both.astype(BF16).reshape(4, 4, 32, 128)
     z_rd = go(rds, rdr, "z")
 
     row = lax.broadcasted_iota(jnp.int32, (8, D), 0)
@@ -500,6 +505,7 @@
     v = jnp.where(row == 4, total(24), v)
     vs[0] = v
     v_z = go(vs.at[0], vs.at[5], "z")
+    z_dxn = go(mrecv.at[:, pl.ds(0, 512)], xr, "z")
 
     turned(perm, dmt, dm)
 
@@ -522,31 +528,27 @@
         tail_gemm(i, 0, lambda cols, t: into(s_t.at[i], cols, t))
         tail[i].e1()
 
-    ffn_keep(2)
-    for i in range(2):
-        ffn[i].f1()
+    def each(lo_, hi_, name):
+        for i in range(lo_, hi_):
+            getattr(ffn[i], name)()
+
+    each(0, 2, "f1")
     tail_keep(0)
     tail_keep(1)
-    for i in range(4, 6):
-        ffn[i].e2()
+    each(2, 4, "f1")
     v_z.wait_recv()
     vs[1] = vs[0] + jnp.where(row < 2, vs[5], 0.0)
     v_c = go(vs.at[1], vs.at[6], "c")
-    for i in range(2, 4):
-        ffn[i].f1()
+    each(0, 2, "f2")
+    each(4, 6, "f1")
     for i in range(2):
         tail[i].e2()
-    for i in range(2):
-        ffn[i].f2()
     v_c.wait_recv()
     vs[2] = vs[1] + vs[6]
     y, zh, x, c = place
     vx[x] = vs[2]
     v_x = [go(vs.at[2], vx.at[x], n) for n in ("xp", "xm", "x2")]
-    for i in range(4, 6):
-        ffn[i].f1()
-    for i in range(2, 4):
-        ffn[i].f2()
+    each(2, 4, "f2")
 
     z_dxn.wait_recv()
     z_rd.wait_recv()
@@ -554,18 +556,14 @@
     def tstep(t):
         rows = pl.ds(mult(t, 64), 64)
         r1 = r1v[rows, 0:1]
-        d = own[rows, :] + xr[rows, :].astype(F32)
-        q = rdr[rows, :].astype(F32)
+        d = dce[rows, :] + xr[rows, :].astype(F32)
+        q = flat(rdr[t // 2, pl.ds(mod(t, 2) * 2, 2)]).astype(F32)
         mean = (rd[rows, 0:1] + q[:, 0:1] + q[:, 64:65]) * (1.0 / D)
         xo = xv[rows, mine].astype(F32)
         tg[rows, :] += r1 * (d * g1[:, mine]) - xo * (r1 * r1 * r1 * mean)
 
     tiles(8, tstep)
-    z_out.wait_recv()
-    bo[...] = (bo[...].astype(F32) + br[...].astype(F32)).astype(BF16)
-
-    for i in range(4, 6):
-        ffn[i].f2()
+    each(4, 6, "f2")
     for i in range(2):
         tail[i].f1()
     for w in v_x:
@@ -573,32 +571,35 @@
     vs[3] = (vx[0] + vx[1]) + (vx[2] + vx[3])
     vy[y] = vs[3]
     v_y = [go(vs.at[3], vy.at[y], n) for n in ("yp", "ym", "y2")]
-    for i in range(6):
-        ffn[i].hop()
+    each(0, 4, "hop")
+    bo[...] = (nn(u[...], wd[:, mine]) + hv[:, mine].astype(F32)).astype(BF16)
     for i in range(2):
         tail[i].f2()
+    each(4, 6, "hop")
     for w in v_y:
         w.wait_recv()
     vs[4] = (vy[0] + vy[1]) + (vy[2] + vy[3])
     v_h = go(vs.at[4], vs.at[7], "zh")
+    for i in range(2):
+        tail[i].hop()
     for i, o in enumerate((gate_o, up_o, down_o)):
         o[:, 0:WF] = ffn[2 * i].result()
         o[:, WF : 2 * WF] = ffn[2 * i + 1].result()
-    for i in range(2):
-        tail[i].hop()
+    z_out.wait_recv()
+    bo[...] = (bo[...].astype(F32) + flat(br[...]).astype(F32)).astype(BF16)
+    v_h.wait_recv()
+    v = vs[4] + vs[7]
+    ng_o[...] = v[0:1, :]
+    fg_o[...] = v[1:2, :]
+    cg_o[...] = v[2:5, 0:512]
     for i in range(2):
         t = tail[i].result()
         out_o[:, 256 * i : 256 * i + 256] = t[:, 0:256]
         for j in range(6):
             n = 768 * i + 128 * j
             in_o[n // 512, :, n % 512 : n % 512 + 128] = t[:, 256 + 128 * j : 384 + 128 * j]
-    v_h.wait_recv()
-    v = vs[4] + vs[7]
-    ng_o[...] = v[0:1, :]
-    fg_o[...] = v[1:2, :]
-    cg_o[...] = v[2:5, 0:512]
     for q in made:
-        if all(q is not d for d in z_m):
+        if all(q is not d for d in (*z_m, back)):
             q.wait_send()
     for q in ffn + tail:
         q.finish()
@@ -631,13 +632,12 @@
         pltpu.VMEM((ROWS + 8, HALF), F32),
         pltpu.VMEM((2, HALF, D), BF16),
         pltpu.VMEM((2, HALF, ROWS), BF16),
-        pltpu.VMEM((ROWS, HALF), F32),
+        pltpu.VMEM((2, HALF, ROWS), BF16),
         pltpu.VMEM((ROWS, HALF), BF16),
         pltpu.VMEM((ROWS, HALF), BF16),
-        pltpu.VMEM((ROWS, HALF), BF16),
+        pltpu.VMEM((4, 4, 32, HALF), BF16),
         pltpu.VMEM((ROWS, 128), F32),
-        pltpu.VMEM((ROWS, 128), BF16),
-        pltpu.VMEM((ROWS, 128), BF16),
+        pltpu.VMEM((4, 4, 32, 128), BF16),
         pltpu.VMEM((ROWS, 128), F32),
         pltpu.VMEM((40, D), F32),
         pltpu.VMEM((8, 8, D), F32),

time: 140 us -> 136 us (0.971)
  Pallas kernels: 139 us -> 134 us
    pallas_call x1, Pallas kernels: 136 us -> 131 us  [block(): pl.pallas_call(block_kernel, out_shape=(sds((ROWS, HALF), BF16), sds((ROW...]
where the time goes in v4:
time: 136 us; the launch traced here: 135 us
  Pallas kernels  134 us (99%)
    pallas_call x1, Pallas kernels, block(): pl.pallas_call(block_kernel, out_shape=(sds((ROWS, HALF), BF16), sds((ROW...  131 us
    pallas_call x1, Pallas kernels, settle(): pl.pallas_call(settle_kernel, out_shape=tuple((jax.ShapeDtypeStruct(a.sha...  2.93 us

profile of v4, /device:TPU:0, one launch (start us, length us, event | category | flops | bytes accessed | tf_op | source)
XLA Modules:
  0.0 135.1 jit_solution(1234346553669470420)
XLA Ops:
  0.6 131.4 %block.1 = (bf16[512,512]{1,0:T(8,128)(2,1)}, f32[512,512]{1,0:T(8,128)}, f32[16,2304]{1,0:T(8,128)}, f32[16,2304]{1,0:T(8,128)}, f32[16,2304]{1,0:T(8,128)}, /*...) custom-call(bf16[512,512]{1,0:T(8,128)(2,1)} %tok_in.1, ...), custom_call_target="tpu_custom_call" | custom-call | flops 32000000000 | bytes 24000000 | tf_op jit(solution)/shard_map/block/pallas_call | solution.py:659
  132.0 2.9 %settle.1 = (bf16[512,512]{1,0:T(8,128)(2,1)}, f32[512,512]{1,0:T(8,128)}, f32[16,2304]{1,0:T(8,128)}, f32[16,2304]{1,0:T(8,128)}, f32[16,2304]{1,0:T(8,128)}, /...) custom-call(bf16[512,512]{1,0:T(8,128)(2,1)} %get-tuple-element.30.re, ...), custom_call_target="tpu_custom_call" | custom-call | tf_op jit(solution)/shard_map/settle/pallas_call | solution.py:695
